TPU v7x, 32 devices: a whole 2x2x4 slice. The times are simulated.
32 devices in a mesh: dp: 8 (over z, y), seq: 4 (over x, core).
Axes of the slice: x: 2, y: 2, z: 4, core: 2. Of those that a mesh axis runs over, the one named last changes fastest.
Arguments:
- layer_input: bfloat16 [16, 2048, 768], P('dp', 'seq'), may hold values from -10 to 10
- cotangent: bfloat16 [16, 2048, 768], P('dp', 'seq'), may hold values from -6 to 6
- attn_master: float32 [768, 4, 768], P('dp'), may hold values from -2.309401 to 2.309401
- up_master: float32 [768, 3072], P('dp'), may hold values from -0.21875 to 0.21875
- down_master: float32 [3072, 768], P('dp'), may hold values from -0.109375 to 0.109375
- norm_params: float32 [4, 768], replicated, may hold values from -1.5 to 2.4
- attn_first: float32 [768, 4, 768], P('dp'), may hold values from -0.005859375 to 0.005859375
- up_first: float32 [768, 3072], P('dp'), may hold values from -0.005859375 to 0.005859375
- down_first: float32 [3072, 768], P('dp'), may hold values from -0.005859375 to 0.005859375
- norm_first: float32 [4, 768], replicated, may hold values from -0.005859375 to 0.005859375
- attn_second: float32 [768, 4, 768], P('dp'), may hold values from 1.4128508e-07 to 5.6514034e-07
- up_second: float32 [768, 3072], P('dp'), may hold values from 1.4128508e-07 to 5.6514034e-07
- down_second: float32 [3072, 768], P('dp'), may hold values from 1.4128508e-07 to 5.6514034e-07
- norm_second: float32 [4, 768], replicated, may hold values from 1.4128508e-07 to 5.6514034e-07
Outputs:
- layer_output: bfloat16 [16, 2048, 768], P('dp', 'seq')
- input_grad: float32 [16, 2048, 768], P('dp', 'seq')
- attn_grad: float32 [768, 4, 768], P('dp')
- up_grad: float32 [768, 3072], P('dp')
- down_grad: float32 [3072, 768], P('dp')
- norm_grad: float32 [4, 768], replicated
- grad_norm: float32 [], replicated
- attn_new: float32 [768, 4, 768], P('dp')
- up_new: float32 [768, 3072], P('dp')
- down_new: float32 [3072, 768], P('dp')
- norm_new: float32 [4, 768], replicated
- attn_first_new: float32 [768, 4, 768], P('dp')
- up_first_new: float32 [768, 3072], P('dp')
- down_first_new: float32 [3072, 768], P('dp')
- norm_first_new: float32 [4, 768], replicated
- attn_second_new: float32 [768, 4, 768], P('dp')
- up_second_new: float32 [768, 3072], P('dp')
- down_second_new: float32 [3072, 768], P('dp')
- norm_second_new: float32 [4, 768], replicated
All inputs are finite; a program needn't handle non-finite values.
Results may differ from a plain program's by a relative error of at most 0.018.
Values may be sent and summed in bfloat16 or wider, within the bound.
A program may use at most 256 MiB of HBM per device.

v0:
```python
import math

import jax
import jax.numpy as jnp
from jax import lax
from jax.sharding import PartitionSpec as P

D = 768
HEAD = 64
FF = 3072
STEP = 5


highest = lax.Precision.HIGHEST
beta_one = 0.5
beta_two = 0.5
learn_rate = 0.02
gain_rate = 0.2
epsilon = 1e-08
weight_decay = 0.01
norm_eps = 1e-05
clip_limit = 1.0


def prefix(part, axis, combine, identity):
    place = lax.axis_index(axis)
    gathered = jax.tree.map(lambda a: lax.all_gather(a, axis), part)
    state = jax.tree.map(lambda a, e: jnp.zeros_like(a) + jnp.asarray(e, a.dtype), part, identity)

    def prefix_one(step, state):
        return combine(
            state, jax.tree.map(lambda a: lax.dynamic_index_in_dim(a, step, 0, False), gathered)
        )

    return lax.fori_loop(0, place, prefix_one, state)


def carried_in(shard, axis, join, neutral):
    count = lax.axis_size(axis)
    place = lax.axis_index(axis)
    ahead = count - 1 - place
    gathered = jax.tree.map(
        lambda a, kind: lax.all_gather(a.astype(kind), axis),
        shard,
        jax.tree.map(lambda a: jnp.bfloat16 if a.dtype == jnp.float32 else a.dtype, shard),
    )
    state = jax.tree.map(lambda a, e: jnp.zeros_like(a) + jnp.asarray(e, a.dtype), shard, neutral)

    def carried_one(step, state):
        source = count - 1 - step
        return join(
            state,
            jax.tree.map(
                lambda a, own: lax.dynamic_index_in_dim(a, source, 0, False).astype(own.dtype),
                gathered,
                shard,
            ),
        )

    return lax.fori_loop(0, ahead, carried_one, state)


def add_states(earlier, later):
    return jax.tree.map(jnp.add, earlier, later)


def layer_norm(values, gain_row, bias_row):
    centered = values - jnp.mean(values, axis=-1, keepdims=True)
    spread = jnp.mean(centered * centered, axis=-1, keepdims=True)
    return centered * lax.rsqrt(spread + norm_eps) * gain_row + bias_row


def piece_scores(query_cos, query_sin, key_cos, key_sin, causal):
    scores = jnp.einsum("ihe,jhe->hij", query_cos, key_cos, preferred_element_type=jnp.float32)
    scores = scores + jnp.einsum(
        "ihe,jhe->hij", query_sin, key_sin, preferred_element_type=jnp.float32
    )
    return jnp.where(causal[None], scores, 0.0)


def adamw(weight, gradient, first_moment, second, step_rate):
    first_new = beta_one * first_moment + (1.0 - beta_one) * gradient
    second_new = beta_two * second + (1.0 - beta_two) * gradient * gradient
    first_hat = first_new / (1.0 - beta_one**STEP)
    second_hat = second_new / (1.0 - beta_two**STEP)
    weight_new = weight - step_rate * (
        first_hat / (jnp.sqrt(second_hat) + epsilon) + weight_decay * weight
    )
    return (weight_new, first_new, second_new)


def shards(
    layer_input,
    cotangent,
    attn_master,
    up_master,
    down_master,
    norm_params,
    attn_first,
    up_first,
    down_first,
    norm_first,
    attn_second,
    up_second,
    down_second,
    norm_second,
):
    groups, piece_rows, model_width = layer_input.shape
    head_count = model_width // HEAD
    length = piece_rows * lax.axis_size("seq")
    rows_all = groups * piece_rows
    attn_full, up_full, down_full = (
        lax.all_gather(attn_master.astype(jnp.bfloat16), "dp", axis=0, tiled=True),
        lax.all_gather(up_master.astype(jnp.bfloat16), "dp", axis=0, tiled=True),
        lax.all_gather(down_master.astype(jnp.bfloat16), "dp", axis=0, tiled=True),
    )
    project_in = attn_full[:, :3, :].reshape(model_width, 3 * model_width)
    out_weight = attn_full[:, 3, :]
    tokens = layer_input.reshape(rows_all, model_width)
    projected = jnp.dot(tokens, project_in, preferred_element_type=jnp.float32)
    query_pre = projected[:, :model_width]
    key_pre = projected[:, model_width : 2 * model_width]
    value_pre = projected[:, 2 * model_width :]
    position = (lax.axis_index("seq") * piece_rows + jnp.arange(piece_rows)).astype(jnp.float32)
    phase_angle = math.pi / 2 * position / length
    cosine_weight = jnp.tile(jnp.cos(phase_angle), groups)[:, None]
    sine_weight = jnp.tile(jnp.sin(phase_angle), groups)[:, None]
    query_feat = jax.nn.softplus(query_pre)
    key_feat = jax.nn.softplus(key_pre)
    shape_four = (groups, piece_rows, head_count, HEAD)
    query_cos = (query_feat * cosine_weight).astype(jnp.bfloat16).reshape(shape_four)
    query_sin = (query_feat * sine_weight).astype(jnp.bfloat16).reshape(shape_four)
    key_cos = (key_feat * cosine_weight).astype(jnp.bfloat16).reshape(shape_four)
    key_sin = (key_feat * sine_weight).astype(jnp.bfloat16).reshape(shape_four)
    values = value_pre.astype(jnp.bfloat16).reshape(shape_four)
    local_state = (
        jnp.stack(
            [
                jnp.einsum("gjhe,gjhf->ghef", key_cos, values, preferred_element_type=jnp.float32),
                jnp.einsum("gjhe,gjhf->ghef", key_sin, values, preferred_element_type=jnp.float32),
            ],
            axis=1,
        ),
        jnp.stack(
            [
                jnp.sum(key_cos, axis=1, dtype=jnp.float32),
                jnp.sum(key_sin, axis=1, dtype=jnp.float32),
            ],
            axis=1,
        ),
    )
    identity = jax.tree.map(jnp.zeros_like, local_state)
    prior_state, prior_total = prefix(
        (local_state[0], local_state[1]), "seq", add_states, (identity[0], identity[1])
    )
    causal = jnp.arange(piece_rows)[:, None] >= jnp.arange(piece_rows)[None, :]
    attended_list = []
    denominator_list = []
    for group_index in range(groups):
        scores = piece_scores(
            query_cos[group_index],
            query_sin[group_index],
            key_cos[group_index],
            key_sin[group_index],
            causal,
        )
        qcos_wide = query_cos[group_index].astype(jnp.float32)
        qsin_wide = query_sin[group_index].astype(jnp.float32)
        numerator = jnp.einsum(
            "hij,jhe->ihe",
            scores.astype(jnp.bfloat16),
            values[group_index],
            preferred_element_type=jnp.float32,
        )
        numerator = numerator + jnp.einsum(
            "ihe,hef->ihf", qcos_wide, prior_state[group_index, 0], precision=highest
        )
        numerator = numerator + jnp.einsum(
            "ihe,hef->ihf", qsin_wide, prior_state[group_index, 1], precision=highest
        )
        denominator = jnp.sum(scores, axis=-1).T
        denominator = denominator + jnp.einsum(
            "ihe,he->ih", qcos_wide, prior_total[group_index, 0], precision=highest
        )
        denominator = denominator + jnp.einsum(
            "ihe,he->ih", qsin_wide, prior_total[group_index, 1], precision=highest
        )
        attended_list.append(numerator / denominator[:, :, None])
        denominator_list.append(denominator)
    attended = jnp.stack(attended_list)
    attended_low = attended.reshape(rows_all, model_width).astype(jnp.bfloat16)
    branch_one = jnp.dot(attended_low, out_weight, preferred_element_type=jnp.float32)
    residual_one = tokens.astype(jnp.float32) + branch_one
    first_norm, norm_one_back = jax.vjp(layer_norm, residual_one, norm_params[0], norm_params[1])
    first_low = first_norm.astype(jnp.bfloat16)
    hidden = jnp.dot(first_low, up_full, preferred_element_type=jnp.float32)
    activated, gelu_back = jax.vjp(jax.nn.gelu, hidden)
    activated_low = activated.astype(jnp.bfloat16)
    branch_two = jnp.dot(activated_low, down_full, preferred_element_type=jnp.float32)
    result, norm_two_back = jax.vjp(
        layer_norm, first_norm + branch_two, norm_params[2], norm_params[3]
    )
    layer_output = result.astype(jnp.bfloat16).reshape(groups, piece_rows, model_width)
    grad_residual_two, grad_gain_two, grad_bias_two = norm_two_back(
        cotangent.reshape(rows_all, model_width).astype(jnp.float32)
    )
    grad_branch_two = grad_residual_two.astype(jnp.bfloat16)
    grad_down = jnp.einsum(
        "nf,nd->fd", activated_low, grad_branch_two, preferred_element_type=jnp.float32
    )
    grad_activated = jnp.einsum(
        "nd,fd->nf", grad_branch_two, down_full, preferred_element_type=jnp.float32
    )
    grad_hidden = gelu_back(grad_activated)[0].astype(jnp.bfloat16)
    grad_up = jnp.einsum("nd,nf->df", first_low, grad_hidden, preferred_element_type=jnp.float32)
    grad_first = grad_residual_two + jnp.einsum(
        "nf,df->nd", grad_hidden, up_full, preferred_element_type=jnp.float32
    )
    grad_residual_one, grad_gain_one, grad_bias_one = norm_one_back(grad_first)
    grad_branch_one = grad_residual_one.astype(jnp.bfloat16)
    grad_out_weight = jnp.einsum(
        "nd,ne->de", attended_low, grad_branch_one, preferred_element_type=jnp.float32
    )
    grad_attended = jnp.einsum(
        "ne,de->nd", grad_branch_one, out_weight, preferred_element_type=jnp.float32
    ).reshape(shape_four)
    grad_qcos_list = []
    grad_qsin_list = []
    grad_kcos_list = []
    grad_ksin_list = []
    grad_values_list = []
    prior_grad_state = []
    prior_grad_total = []
    for group_index in range(groups):
        denominator = denominator_list[group_index]
        grad_numerator = (grad_attended[group_index] / denominator[:, :, None]).astype(jnp.bfloat16)
        grad_denominator = (
            -jnp.sum(grad_attended[group_index] * attended[group_index], axis=-1) / denominator
        )
        scores = piece_scores(
            query_cos[group_index],
            query_sin[group_index],
            key_cos[group_index],
            key_sin[group_index],
            causal,
        )
        grad_scores = (
            jnp.einsum(
                "ihe,jhe->hij",
                grad_numerator,
                values[group_index],
                preferred_element_type=jnp.float32,
            )
            + grad_denominator.T[:, :, None]
        )
        grad_scores = jnp.where(causal[None], grad_scores, 0.0).astype(jnp.bfloat16)
        grad_numerator_wide = grad_numerator.astype(jnp.float32)
        grad_qcos = jnp.einsum(
            "hij,jhe->ihe", grad_scores, key_cos[group_index], preferred_element_type=jnp.float32
        )
        grad_qcos = grad_qcos + jnp.einsum(
            "ihf,hef->ihe", grad_numerator_wide, prior_state[group_index, 0], precision=highest
        )
        grad_qcos = grad_qcos + grad_denominator[:, :, None] * prior_total[group_index, 0][None]
        grad_qsin = jnp.einsum(
            "hij,jhe->ihe", grad_scores, key_sin[group_index], preferred_element_type=jnp.float32
        )
        grad_qsin = grad_qsin + jnp.einsum(
            "ihf,hef->ihe", grad_numerator_wide, prior_state[group_index, 1], precision=highest
        )
        grad_qsin = grad_qsin + grad_denominator[:, :, None] * prior_total[group_index, 1][None]
        grad_qcos_list.append(grad_qcos)
        grad_qsin_list.append(grad_qsin)
        grad_kcos_list.append(
            jnp.einsum(
                "hij,ihe->jhe",
                grad_scores,
                query_cos[group_index],
                preferred_element_type=jnp.float32,
            )
        )
        grad_ksin_list.append(
            jnp.einsum(
                "hij,ihe->jhe",
                grad_scores,
                query_sin[group_index],
                preferred_element_type=jnp.float32,
            )
        )
        grad_values_list.append(
            jnp.einsum(
                "hij,ihe->jhe",
                scores.astype(jnp.bfloat16),
                grad_numerator,
                preferred_element_type=jnp.float32,
            )
        )
        prior_grad_state.append(
            jnp.stack(
                [
                    jnp.einsum(
                        "ihe,ihf->hef",
                        query_cos[group_index],
                        grad_numerator,
                        preferred_element_type=jnp.float32,
                    ),
                    jnp.einsum(
                        "ihe,ihf->hef",
                        query_sin[group_index],
                        grad_numerator,
                        preferred_element_type=jnp.float32,
                    ),
                ]
            )
        )
        prior_grad_total.append(
            jnp.stack(
                [
                    jnp.einsum(
                        "ihe,ih->he",
                        query_cos[group_index].astype(jnp.float32),
                        grad_denominator,
                        precision=highest,
                    ),
                    jnp.einsum(
                        "ihe,ih->he",
                        query_sin[group_index].astype(jnp.float32),
                        grad_denominator,
                        precision=highest,
                    ),
                ]
            )
        )
    later_state, later_total = carried_in(
        (jnp.stack(prior_grad_state), jnp.stack(prior_grad_total)),
        "seq",
        add_states,
        (identity[0], identity[1]),
    )
    values_wide = values.astype(jnp.float32)
    kcos_wide = key_cos.astype(jnp.float32)
    ksin_wide = key_sin.astype(jnp.float32)
    grad_kcos = (
        jnp.stack(grad_kcos_list)
        + jnp.einsum("gjhf,ghef->gjhe", values_wide, later_state[:, 0], precision=highest)
        + later_total[:, 0][:, None]
    )
    grad_ksin = (
        jnp.stack(grad_ksin_list)
        + jnp.einsum("gjhf,ghef->gjhe", values_wide, later_state[:, 1], precision=highest)
        + later_total[:, 1][:, None]
    )
    grad_values = jnp.stack(grad_values_list)
    grad_values = grad_values + jnp.einsum(
        "gjhe,ghef->gjhf", kcos_wide, later_state[:, 0], precision=highest
    )
    grad_values = grad_values + jnp.einsum(
        "gjhe,ghef->gjhf", ksin_wide, later_state[:, 1], precision=highest
    )
    grad_query = (
        jnp.stack(grad_qcos_list).reshape(rows_all, model_width) * cosine_weight
        + jnp.stack(grad_qsin_list).reshape(rows_all, model_width) * sine_weight
    )
    grad_keys = (
        grad_kcos.reshape(rows_all, model_width) * cosine_weight
        + grad_ksin.reshape(rows_all, model_width) * sine_weight
    )
    grad_projected = jnp.concatenate(
        [
            (grad_query * jax.nn.sigmoid(query_pre)).astype(jnp.bfloat16),
            (grad_keys * jax.nn.sigmoid(key_pre)).astype(jnp.bfloat16),
            grad_values.reshape(rows_all, model_width).astype(jnp.bfloat16),
        ],
        axis=1,
    )
    input_grad = grad_residual_one + jnp.einsum(
        "nk,dk->nd", grad_projected, project_in, preferred_element_type=jnp.float32
    )
    input_grad = input_grad.reshape(groups, piece_rows, model_width)
    grad_in = jnp.einsum("nd,nk->dk", tokens, grad_projected, preferred_element_type=jnp.float32)
    grad_attn = jnp.concatenate(
        [grad_in.reshape(model_width, 3, model_width), grad_out_weight[:, None, :]], axis=1
    )
    norm_grad_local = jnp.stack([grad_gain_one, grad_bias_one, grad_gain_two, grad_bias_two])
    norm_grad_raw = lax.psum(norm_grad_local, ("dp", "seq"))
    row_blocks = (
        lax.psum_scatter(
            grad_attn.astype(jnp.bfloat16), "dp", scatter_dimension=0, tiled=True
        ).astype(jnp.float32),
        lax.psum_scatter(
            grad_up.astype(jnp.bfloat16), "dp", scatter_dimension=0, tiled=True
        ).astype(jnp.float32),
        lax.psum_scatter(
            grad_down.astype(jnp.bfloat16), "dp", scatter_dimension=0, tiled=True
        ).astype(jnp.float32),
    )
    shard_attn, shard_up, shard_down = (
        lax.psum(row_blocks[0].astype(jnp.bfloat16), "seq").astype(jnp.float32),
        lax.psum(row_blocks[1].astype(jnp.bfloat16), "seq").astype(jnp.float32),
        lax.psum(row_blocks[2].astype(jnp.bfloat16), "seq").astype(jnp.float32),
    )
    local_square = (
        jnp.sum(shard_attn * shard_attn)
        + jnp.sum(shard_up * shard_up)
        + jnp.sum(shard_down * shard_down)
    )
    square = lax.psum(local_square, "dp") + jnp.sum(norm_grad_raw * norm_grad_raw)
    grad_norm = jnp.sqrt(square)
    clip_scale = clip_limit / jnp.maximum(grad_norm, clip_limit)
    attn_grad = shard_attn * clip_scale
    up_grad = shard_up * clip_scale
    down_grad = shard_down * clip_scale
    norm_grad = norm_grad_raw * clip_scale
    attn_rate = (
        learn_rate * jnp.array([1.0, 1.0, 1.0, math.sqrt(length // 8)], jnp.float32)[None, :, None]
    )
    attn_new, attn_first_new, attn_second_new = adamw(
        attn_master, attn_grad, attn_first, attn_second, attn_rate
    )
    up_new, up_first_new, up_second_new = adamw(up_master, up_grad, up_first, up_second, learn_rate)
    down_new, down_first_new, down_second_new = adamw(
        down_master, down_grad, down_first, down_second, learn_rate * math.sqrt(D / FF)
    )
    norm_new, norm_first_new, norm_second_new = adamw(
        norm_params, norm_grad, norm_first, norm_second, gain_rate
    )
    return (
        layer_output,
        input_grad,
        attn_grad,
        up_grad,
        down_grad,
        norm_grad,
        grad_norm,
        attn_new,
        up_new,
        down_new,
        norm_new,
        attn_first_new,
        up_first_new,
        down_first_new,
        norm_first_new,
        attn_second_new,
        up_second_new,
        down_second_new,
        norm_second_new,
    )


def solution(mesh):
    in_specs = (
        P("dp", "seq", None),
        P("dp", "seq", None),
        P("dp", None, None),
        P("dp", None),
        P("dp", None),
        P(),
        P("dp", None, None),
        P("dp", None),
        P("dp", None),
        P(),
        P("dp", None, None),
        P("dp", None),
        P("dp", None),
        P(),
    )
    out_specs = (
        P("dp", "seq", None),
        P("dp", "seq", None),
        P("dp", None, None),
        P("dp", None),
        P("dp", None),
        P(),
        P(),
        P("dp", None, None),
        P("dp", None),
        P("dp", None),
        P(),
        P("dp", None, None),
        P("dp", None),
        P("dp", None),
        P(),
        P("dp", None, None),
        P("dp", None),
        P("dp", None),
        P(),
    )
    return jax.shard_map(shards, mesh=mesh, in_specs=in_specs, out_specs=out_specs, check_vma=False)
```

profile of v0, /device:TPU:0, one launch (start us, length us, event | category | flops | bytes accessed | tf_op | source)
XLA Modules:
  0.0 1029.5 jit_solution(16202857127287533490)
XLA Ops:
  9.7 83.7 %all-gather.8.cloned.1.call-done = bf16[768,4,768]{2,1,0:T(4,128)(2,1)} async-done(((bf16[96,4,768]{2,1,0:T(4,128)(2,1)}), bf16[768,4,768]{2,1,0:T(4,128)(2,1)}) %all-gather.8.cloned.1.call-update) | async-done | bytes 4718608 | tf_op jit(solution)/shard_map/all_gather | solution.py:113
  93.4 6.5 copy.405
  99.9 8.6 fusion.103
  108.5 5.7 multiply_convert_fusion.3
  118.8 3.2 slice.197
  124.7 3.9 reshape.293
  171.2 7.6 fusion.109
  178.9 6.4 fusion.108
  185.3 6.4 fusion.106
  191.8 20.2 %fusion.9 = (f32[12,512]{1,0:T(8,128)}, f32[12,512]{1,0:T(8,128)}, bf16[12,512,512]{1,2,0:T(8,128)(2,1)}, bf16[12,512,512]{1,2,0:T(8,128)(2,1)}) fusion(f32[12,512,512]{1,2,0:T(8,128)} %fusion.106, pred[512,512]{0,1:T(8,128)(4,1)} %iota_compare_fusion, f32[12,512,512]{1,2,0:T(8,128)} %fusion.108, f32[12,512,512]{1,2,0:T(8,128)} %fusion.109, ...), kind=kOutput, calls=%fused_computation.33 | convolution fusion | flops 427806720 | bytes 52215808 | tf_op jit(solution)/shard_map/ihe,jhe->hij/dot_general | solution.py:74
  211.9 5.3 fusion.107
  221.2 6.5 slice.207
  227.7 5.3 all-gather.1
  250.9 14.1 %all-gather.10.cloned.1.call-done = bf16[768,3072]{1,0:T(8,128)(2,1)} async-done(((bf16[96,3072]{1,0:T(8,128)(2,1)}), bf16[768,3072]{1,0:T(8,128)(2,1)}) %all-gather.10.cloned.1.call-update) | async-done | bytes 4718608 | tf_op jit(solution)/shard_map/all_gather | solution.py:114
  265.0 11.3 %fusion.89 = f32[1024,3072]{1,0:T(8,128)} fusion(bf16[768,3072]{1,0:T(8,128)(2,1)} %all-gather.10.cloned.1.call-done, f32[1024,768]{1,0:T(8,128)} %copy-done.28, f32[768]{0:T(1024)S(1)} %get-tuple-element.194, f32[768]{0:T(1024)S(1)} %get-tuple-element.195, f32[1024]{0:T(1024)S(1)} %fusion.80, f32[1024]{0:T(1024)S(1)} %broadcast_multiply_fusion.2), kind=kOutput, calls=%fused_computation.232 | convolution fusion | flops 4835770368 | bytes 20461568 | tf_op jit(solution)/shard_map/dot_general | solution.py:196
  276.3 69.4 %all-gather.12.cloned.1.call-done = bf16[3072,768]{1,0:T(8,128)(2,1)} async-done(((bf16[384,768]{1,0:T(8,128)(2,1)}), bf16[3072,768]{1,0:T(8,128)(2,1)}) %all-gather.12.cloned.1.call-update) | async-done | bytes 4718608 | tf_op jit(solution)/shard_map/all_gather | solution.py:115
  345.7 12.5 %fusion.105 = (f32[1024]{0:T(1024)S(1)}, f32[1024,768]{1,0:T(8,128)S(1)}) fusion(bf16[3072,768]{1,0:T(8,128)(2,1)} %all-gather.12.cloned.1.call-done, f32[1024,3072]{1,0:T(8,128)} %fusion.89, f32[768]{0:T(1024)S(1)} %get-tuple-element.194, f32[768]{0:T(1024)S(1)} %get-tuple-element.195, f32[1024]{0:T(1024)S(1)} %fusion.80, f32[1024,768]{1,0:T(8,128)} %copy-done.28, ...), kind=kOutput, calls=%fused_computation.243 | convolution fusion | flops 4864867328 | bytes 23611392 | tf_op jit(solution)/shard_map/dot_general | solution.py:199
  363.9 16.4 %fusion.8 = bf16[1024,3072]{1,0:T(8,128)(2,1)} fusion(f32[1024,3072]{1,0:T(8,128)} %fusion.89, bf16[3072,768]{1,0:T(8,128)(2,1)} %all-gather.12.cloned.1.call-done, f32[1024,768]{1,0:T(8,128)S(1)} %get-tuple-element.243, f32[1024]{0:T(1024)S(1)} %negate_multiply_fusion.1), kind=kOutput, calls=%fused_computation.18 | convolution fusion | flops 4896325632 | bytes 26742784 | tf_op jit(solution)/shard_map/nd,fd->nf/dot_general | solution.py:211
  380.3 10.1 multiply_reduce_fusion
  402.5 3.2 convolution_bitcast_fusion.5
  435.9 3.7 copy.337
  439.6 4.3 copy.342
  446.4 3.6 copy.343
  450.0 4.7 copy.367
  454.7 5.2 all_gather.37
  459.9 6.1 convolution_bitcast_fusion.4
  469.2 3.2 convolution_bitcast_fusion.2
  472.4 6.1 convolution_bitcast_fusion.1
  478.5 3.2 convolution_bitcast_fusion
  481.9 5.4 while.27
  497.2 3.7 copy.351
  508.8 3.9 copy.357
  512.7 4.5 fusion.16
  523.1 6.7 multiply_convert_fusion.2
  529.8 6.4 convolution_convert_fusion.2
  536.3 8.6 copy.366
  544.9 9.3 pad_maximum_fusion.1
  556.0 12.9 %convolution_convert_fusion = bf16[3072,768]{1,0:T(8,128)(2,1)} fusion(f32[1024,768]{1,0:T(8,128)S(1)} %copy-done.63, f32[1024]{0:T(1024)S(1)} %negate_multiply_fusion.1, f32[1024,3072]{1,0:T(8,128)} %fusion.89), kind=kOutput, calls=%fused_computation.26 | convolution fusion | flops 4864081920 | bytes 20451328 | tf_op jit(solution)/shard_map/nf,nd->fd/dot_general | solution.py:208
  570.9 9.9 convolution_convert_fusion.1
  582.6 138.6 %all-reduce.5.cloned.1.call-done = bf16[768,4,768]{2,1,0:T(4,128)(2,1)} async-done(((bf16[768,4,768]{2,1,0:T(4,128)(2,1)}), bf16[768,4,768]{2,1,0:T(4,128)(2,1)}) %all-reduce.5.cloned.1.call-update) | async-done | bytes 4718608
  723.3 95.8 %reduce-scatter.5.cloned.1.call-done = bf16[384,768]{1,0:T(8,128)(2,1)} async-done(((bf16[3072,768]{1,0:T(8,128)(2,1)}), bf16[384,768]{1,0:T(8,128)(2,1)}) %reduce-scatter.5.cloned.1.call-update) | async-done | bytes 589840 | tf_op jit(solution)/shard_map/reduce_scatter | solution.py:393
  819.1 98.7 %reduce-scatter.3.cloned.1.call-done = bf16[96,3072]{1,0:T(8,128)(2,1)} async-done(((bf16[768,3072]{1,0:T(8,128)(2,1)}), bf16[96,3072]{1,0:T(8,128)(2,1)}) %reduce-scatter.3.cloned.1.call-update) | async-done | bytes 589840 | tf_op jit(solution)/shard_map/reduce_scatter | solution.py:390
  918.2 40.7 %psum.39 = f32[4,768]{1,0:T(4,128)S(1)} all-reduce(f32[4,768]{1,0:T(4,128)S(1)} %pad_maximum_fusion.12), channel_id=1, replica_groups=mesh['dp'=8,'seq'=4] {'dp','seq'}, use_global_device_ids=true, to_apply=%region_32.33 | all-reduce | flops 3072 | bytes 24576 | tf_op jit(solution)/shard_map/psum | solution.py:385
  959.5 8.5 all-reduce.7.cloned.1.call-done
  976.3 9.5 add_add_fusion.2
  985.7 21.8 %psum.38 = f32[]{:T(128)} all-reduce(f32[]{:T(128)S(6)} %add.417), channel_id=1, replica_groups=mesh['dp'=8,'seq'=4] {'dp'}, use_global_device_ids=true, to_apply=%region_27.28 | all-reduce | flops 1 | bytes 8 | tf_op jit(solution)/shard_map/psum | solution.py:407
  1009.6 4.3 multiply_subtract_fusion
  1017.8 3.6 multiply_subtract_fusion.2
  (389 shorter events, 174.4 us)
Async XLA Ops:
  7.2 86.2 %all-gather.8.cloned.1.call-start = ((), (), s32[]{:S(2)}) async-start(), calls=%async_computation.2 | async-start | bytes 5308416 | tf_op jit(solution)/shard_map/all_gather | solution.py:113
  9.5 223.5 %all-gather.16.cloned.1.call-start = ((), (), s32[]{:S(2)}) async-start(), calls=%async_computation.8 | async-start | bytes 7864320 | tf_op jit(solution)/shard_map/all_gather | solution.py:27
  9.7 98.8 %copy-start.84 = (f32[1,4,2,128]{3,1,2,0:T(4,128)}, f32[1,4,2,128]{3,1,2,0:T(4,128)S(1)}, u32[]{:S(2)}) copy-start(f32[1,4,2,128]{3,1,2,0:T(4,128)S(1)} %copy.407) | copy-start | bytes 12292
  9.7 98.8 %copy-start.86 = (f32[1,4,2,128]{3,1,2,0:T(4,128)}, f32[1,4,2,128]{3,1,2,0:T(4,128)S(1)}, u32[]{:S(2)}) copy-start(f32[1,4,2,128]{3,1,2,0:T(4,128)S(1)} %copy.408) | copy-start | bytes 12292
  99.9 8.6 copy-start.58
  108.5 5.7 copy-start.10
  118.8 28.6 %copy-start.14 = (bf16[2,512,12,64]{1,0,3,2:T(2,128)(2,1)}, bf16[2,512,12,64]{1,0,3,2:T(2,128)(2,1)S(1)}, u32[]{:S(2)}) copy-start(bf16[2,512,12,64]{1,0,3,2:T(2,128)(2,1)S(1)} %reshape.292) | copy-start | bytes 4718596
  122.0 6.6 copy-start.18
  137.7 127.4 %all-gather.10.cloned.1.call-start = ((), (), s32[]{:S(2)}) async-start(), calls=%async_computation.3 | async-start | bytes 5308416 | tf_op jit(solution)/shard_map/all_gather | solution.py:114
  139.9 6.3 copy-start.17
  139.9 205.8 %all-gather.12.cloned.1.call-start = ((), (), s32[]{:S(2)}) async-start(), calls=%async_computation.4 | async-start | bytes 5308416 | tf_op jit(solution)/shard_map/all_gather | solution.py:115
  142.2 339.5 %all-gather.14.cloned.1.call-start = ((), (), s32[]{:S(2)}) async-start(), calls=%async_computation.5 | async-start | bytes 3932160 | tf_op jit(solution)/shard_map/all_gather | solution.py:43
  143.3 202.4 %copy-start.91 = (f32[768]{0:T(1024)}, f32[768]{0:T(1024)S(1)}, u32[]{:S(2)}) copy-start(f32[768]{0:T(1024)S(1)} %get-tuple-element.194) | copy-start | bytes 9220
  154.0 17.2 %copy-start.2 = (bf16[512,768]{0,1:T(8,128)(2,1)}, bf16[512,768]{0,1:T(8,128)(2,1)S(1)}, u32[]{:S(2)}) copy-start(bf16[512,768]{0,1:T(8,128)(2,1)S(1)} %copy.323) | copy-start | bytes 2359300
  161.7 23.6 %copy-start.6 = (bf16[512,768]{0,1:T(8,128)(2,1)}, bf16[512,768]{0,1:T(8,128)(2,1)S(1)}, u32[]{:S(2)}) copy-start(bf16[512,768]{0,1:T(8,128)(2,1)S(1)} %copy.304) | copy-start | bytes 2359300
  171.2 7.7 copy-start.32
  178.9 6.4 copy-start.34
  185.3 6.4 copy-start.36
  191.7 20.2 %copy-start.43 = (bf16[512,768]{0,1:T(8,128)(2,1)S(1)}, bf16[512,768]{0,1:T(8,128)(2,1)}, u32[]{:S(2)}) copy-start(bf16[512,768]{0,1:T(8,128)(2,1)} %copy.301) | copy-start | bytes 2359300
  233.4 5.8 copy-start.80
  363.9 16.4 %copy-start.62 = (f32[1024,768]{1,0:T(8,128)}, f32[1024,768]{1,0:T(8,128)S(1)}, u32[]{:S(2)}) copy-start(f32[1024,768]{1,0:T(8,128)S(1)} %get-tuple-element.243) | copy-start | bytes 9437188
  363.9 16.4 %copy-start.29 = (f32[1024,768]{1,0:T(8,128)S(1)}, f32[1024,768]{1,0:T(8,128)}, u32[]{:S(2)}) copy-start(f32[1024,768]{1,0:T(8,128)} %copy-done.28) | copy-start | bytes 9437188
  392.2 25.9 %copy-start.61 = (f32[1024,768]{1,0:T(8,128)}, f32[1024,768]{1,0:T(8,128)S(1)}, u32[]{:S(2)}) copy-start(f32[1024,768]{1,0:T(8,128)S(1)} %get-tuple-element.241) | copy-start | bytes 9437188
  421.9 299.3 %all-reduce.5.cloned.1.call-start = ((), (), s32[]{:S(2)}) async-start(), calls=%async_computation.9 | async-start | bytes 9437184
  446.4 19.6 %copy-start.9 = (bf16[512,768]{0,1:T(8,128)(2,1)S(1)}, bf16[512,768]{0,1:T(8,128)(2,1)}, u32[]{:S(2)}) copy-start(bf16[512,768]{0,1:T(8,128)(2,1)} %copy-done.6) | copy-start | bytes 2359300
  450.0 16.0 %slice-start = ((s8[6291456]{0:T(1024)(128)(4,1)}), s8[2097152]{0:T(1024)(128)(4,1)S(1)}, s32[]{:S(2)}) async-start(s8[6291456]{0:T(1024)(128)(4,1)} %bitcast.385), calls=%async_computation.11 | async-start | bytes 4194304
  459.9 6.1 slice-start.1
  459.9 9.3 slice-start.2
  469.2 9.3 slice-start.6
  472.4 6.1 slice-start.7
  523.1 6.7 copy-start.72
  523.1 6.7 copy-start.97
  529.8 6.5 copy-start.69
  529.8 6.5 copy-start.71
  536.3 8.6 copy-start.40
  554.2 265.0 %reduce-scatter.5.cloned.1.call-start = ((), (), s32[]{:S(2)}) async-start(), calls=%async_computation.7 | async-start | bytes 5308416 | tf_op jit(solution)/shard_map/reduce_scatter | solution.py:393
  569.0 348.8 %reduce-scatter.3.cloned.1.call-start = ((), (), s32[]{:S(2)}) async-start(), calls=%async_computation.6 | async-start | bytes 5308416 | tf_op jit(solution)/shard_map/reduce_scatter | solution.py:390
  580.7 337.1 %copy-start.20 = (bf16[2,512,768]{2,1,0:T(8,128)(2,1)S(1)}, bf16[2,512,768]{2,1,0:T(8,128)(2,1)}, u32[]{:S(2)}) copy-start(bf16[2,512,768]{2,1,0:T(8,128)(2,1)} %param.20) | copy-start | bytes 4718596
  580.8 337.4 %copy-start.94 = (f32[768]{0:T(1024)S(1)}, f32[768]{0:T(1024)}, u32[]{:S(2)}) copy-start(f32[768]{0:T(1024)} %get-tuple-element.186) | copy-start | bytes 9220
  580.8 337.4 %copy-start.93 = (f32[768]{0:T(1024)S(1)}, f32[768]{0:T(1024)}, u32[]{:S(2)}) copy-start(f32[768]{0:T(1024)} %get-tuple-element.190) | copy-start | bytes 9220
  580.8 337.4 %copy-start.88 = (f32[768]{0:T(1024)S(1)}, f32[768]{0:T(1024)}, u32[]{:S(2)}) copy-start(f32[768]{0:T(1024)} %get-tuple-element.188) | copy-start | bytes 9220
  580.8 387.2 %all-reduce.7.cloned.1.call-start = ((), (), s32[]{:S(2)}) async-start(), calls=%async_computation.10 | async-start | bytes 3538944 | tf_op jit(solution)/shard_map/psum | solution.py:398
  582.6 393.6 %copy-start.70 = (bf16[1024,768]{1,0:T(8,128)(2,1)S(1)}, bf16[1024,768]{1,0:T(8,128)(2,1)}, u32[]{:S(2)}) copy-start(bf16[1024,768]{1,0:T(8,128)(2,1)} %copy-done.69) | copy-start | bytes 4718596
  976.2 32.7 %copy-start.83 = (f32[4,768]{1,0:T(4,128)S(1)}, f32[4,768]{1,0:T(4,128)}, u32[]{:S(2)}) copy-start(f32[4,768]{1,0:T(4,128)} %param.24) | copy-start | bytes 36868
  976.2 32.7 %copy-start.89 = (f32[4,768]{1,0:T(4,128)S(1)}, f32[4,768]{1,0:T(4,128)}, u32[]{:S(2)}) copy-start(f32[4,768]{1,0:T(4,128)} %param.28) | copy-start | bytes 36868
  976.2 32.7 %copy-start.90 = (f32[4,768]{1,0:T(4,128)S(1)}, f32[4,768]{1,0:T(4,128)}, u32[]{:S(2)}) copy-start(f32[4,768]{1,0:T(4,128)} %param.32) | copy-start | bytes 36868
  976.2 33.3 %copy-start.55 = (f32[384,768]{1,0:T(8,128)S(1)}, f32[384,768]{1,0:T(8,128)}, u32[]{:S(2)}) copy-start(f32[384,768]{1,0:T(8,128)} %param.23) | copy-start | bytes 3538948
  976.3 33.3 %copy-start.66 = (bf16[384,768]{1,0:T(8,128)(2,1)S(1)}, bf16[384,768]{1,0:T(8,128)(2,1)}, u32[]{:S(2)}) copy-start(bf16[384,768]{1,0:T(8,128)(2,1)} %get-tuple-element.223) | copy-start | bytes 1769476
  (68 other events, 206.8 us)
Sparse Core Ops, SparseCore 0:
  10.8 82.5 all-gather.7
  137.8 44.5 all-gather.15
  185.1 79.8 all-gather.9
  267.6 78.0 all-gather.11
  422.1 26.6 all-gather.13
  554.3 166.8 all-reduce.4
  724.8 94.2 reduce-scatter.4
  822.8 94.9 reduce-scatter.2
  921.0 47.0 all-reduce.6
where the time goes:
time: 1040 us; the launch traced here: 1030 us
  waiting for transfers between devices  509 us (49%)
  matrix products  223 us (21%)
  local copies, waits for them, and re-layouts  133 us (13%)
  blocking collectives  73 us (7%)
  other arithmetic  68.6 us (7%)
  between operations  20.9 us (2%)
    unnamed x10, waiting for transfers between devices  139 us
    reduce_scatter x1, waiting for transfers between devices, shards(): lax.psum_scatter(grad_up.astype(jnp.bfloat16), 'dp', scatter_dimension=0,...  98.7 us
    reduce_scatter x1, waiting for transfers between devices, shards(): lax.psum_scatter(grad_down.astype(jnp.bfloat16), 'dp', scatter_dimension=...  95.8 us
    all_gather x1, waiting for transfers between devices, shards(): lax.all_gather(attn_master.astype(jnp.bfloat16), 'dp', axis=0, tiled=True)  83.7 us
    all_gather x1, waiting for transfers between devices, shards(): lax.all_gather(down_master.astype(jnp.bfloat16), 'dp', axis=0, tiled=True)  69.4 us
    psum x1, blocking collectives, shards(): norm_grad_raw = lax.psum(norm_grad_local, ('dp', 'seq'))  40.7 us
    unnamed x227, local copies, waits for them, and re-layouts  32.9 us
    dot_general x2, matrix products, piece_scores(): jnp.einsum('ihe,jhe->hij', query_cos, key_cos, preferred_element_type=jnp...  26.6 us
  transfers between devices with their start and end apart: 9, of which 7 were waited for; matrix products, arithmetic and copies ran while one was open for 19% of the time, Pallas kernels for 0%

commit v1 on v0

--- a/solution.py
+++ b/solution.py
@@ -1,8 +1,12 @@
+import functools
 import math
 
 import jax
 import jax.numpy as jnp
+import numpy as np
 from jax import lax
+from jax.experimental import pallas as pl
+from jax.experimental.pallas import tpu as pltpu
 from jax.sharding import PartitionSpec as P
 
 D = 768
@@ -22,6 +26,1419 @@
 clip_limit = 1.0
 
 
+MESH = pl.DeviceIdType.MESH
+f32, bf16 = jnp.float32, jnp.bfloat16
+PIECE = 512
+PAIR = 2 * HEAD
+PLANES = 4
+VMEM_BYTES = 63 * 1024 * 1024
+
+
+def dot(left, right):
+    return jnp.dot(left, right, preferred_element_type=f32)
+
+
+def dot_nt(left, right):
+    return lax.dot_general(left, right, (((1,), (1,)), ((), ())), preferred_element_type=f32)
+
+
+def dot_tn(left, right):
+    return lax.dot_general(left, right, (((0,), (0,)), ((), ())), preferred_element_type=f32)
+
+
+def first_half(shape):
+    return lax.broadcasted_iota(jnp.int32, shape, 1) < HEAD
+
+
+def top_half(shape):
+    return lax.broadcasted_iota(jnp.int32, shape, 0) < HEAD
+
+
+def own_head(value, head):
+    mask = first_half(value.shape)
+    zero = jnp.zeros_like(value)
+    return jnp.where(mask, value, zero) if head == 0 else jnp.where(mask, zero, value)
+
+
+def two_heads(first, second):
+    return jnp.where(first_half(first.shape), first, second)
+
+
+def pair_mask(shape):
+    return (lax.broadcasted_iota(jnp.int32, shape, 1) & (PAIR - 1)) < HEAD
+
+
+def stack_heads(value):
+    mask, zero = pair_mask(value.shape), jnp.zeros_like(value)
+    return jnp.concatenate([jnp.where(mask, value, zero), jnp.where(mask, zero, value)], axis=0)
+
+
+def join_heads(stacked):
+    first, second = stacked[: stacked.shape[0] // 2], stacked[stacked.shape[0] // 2 :]
+    return jnp.where(pair_mask(first.shape), first, second)
+
+
+def side_by_side(wide):
+    half = wide.shape[1] // 2
+    return jnp.concatenate([wide[:, :half], wide[:, half:]], axis=0)
+
+
+def fill_triangles(tri_s):
+    half = tri_s.shape[1]
+    row = lax.broadcasted_iota(jnp.int32, (half, half), 0)
+    col = lax.broadcasted_iota(jnp.int32, (half, half), 1)
+    tri_s[0:half] = (row >= col).astype(f32).astype(bf16)
+    tri_s[half:] = (row <= col).astype(f32).astype(bf16)
+
+
+def causal_product(own, other, right, tri_s):
+    half = PIECE // 2
+    tri = jnp.concatenate([tri_s[0:half], tri_s[0:half]], axis=0)
+    tops, lows = stack_heads(own[0:half]), stack_heads(own[half:])
+    first = dot_nt(jnp.concatenate([tops, lows], axis=0), other[0:half]).astype(bf16)
+    near = dot_nt(lows, other[half:]).astype(bf16) * tri
+    first = jnp.concatenate([first[:PIECE] * tri, first[PIECE:]], axis=0)
+    out = dot(first, right[0:half])
+    low = out[PIECE:] + dot(near, right[half:])
+    return jnp.concatenate([join_heads(out[:PIECE]), join_heads(low)], axis=0)
+
+
+def causal_transposed(own, other, right, tri_s):
+    half = PIECE // 2
+    tri = jnp.concatenate([tri_s[half:], tri_s[half:]], axis=1)
+    top = dot_nt(other[0:half], stack_heads(own[0:half])).astype(bf16) * tri
+    low = dot_nt(other, stack_heads(own[half:])).astype(bf16)
+    low = jnp.concatenate([low[0:half], low[half:] * tri], axis=0)
+    out = dot(side_by_side(low), right[half:])
+    more = dot(side_by_side(top), right[0:half])
+    first = jnp.concatenate([out[0:half] + more[0:half], out[half:PIECE]], axis=0)
+    second = jnp.concatenate([out[PIECE : PIECE + half] + more[half:], out[PIECE + half :]], axis=0)
+    return jnp.where(pair_mask(first.shape), first, second)
+
+
+def with_ones(value):
+    return jnp.concatenate([value, jnp.ones_like(value)], axis=1)
+
+
+def turned(value, trig):
+    wide = value.astype(f32)
+    cos, sin = trig[:, :PAIR], trig[:, PAIR:]
+    return jnp.concatenate([(wide * cos).astype(bf16), (wide * sin).astype(bf16)], axis=1)
+
+
+def squeeze_state(state, totals):
+    cos = two_heads(state[0:HEAD], state[HEAD : 2 * HEAD])
+    sin = two_heads(state[2 * HEAD : 3 * HEAD], state[3 * HEAD :])
+    row = lax.broadcasted_iota(jnp.int32, (16, PAIR), 0)
+    sums = jnp.where(row == 0, totals[:, :PAIR], totals[:, PAIR:])
+    return jnp.concatenate([cos, sin, sums], axis=0)
+
+
+def spread_state(packed):
+    cos, sin = packed[0:HEAD], packed[HEAD:PAIR]
+    state = jnp.concatenate(
+        [own_head(cos, 0), own_head(cos, 1), own_head(sin, 0), own_head(sin, 1)], axis=0
+    )
+    row = lax.broadcasted_iota(jnp.int32, (16, PAIR), 0)
+    sums = packed[PAIR:]
+    ones = jnp.ones((16, PAIR), bf16)
+    blocks = []
+    for kind in range(2):
+        column = dot_tn(jnp.where(row == kind, sums, jnp.zeros_like(sums)), ones).astype(bf16)
+        blocks += [own_head(column[0:HEAD], 0), own_head(column[HEAD:], 1)]
+    return jnp.concatenate([state, jnp.concatenate(blocks, axis=0)], axis=1)
+
+
+def normed(value):
+    centered = value - jnp.mean(value, axis=-1, keepdims=True)
+    rstd = lax.rsqrt(jnp.mean(centered * centered, axis=-1, keepdims=True) + norm_eps)
+    return centered * rstd, rstd
+
+
+def norm_back(grad, unit, rstd):
+    mean = jnp.mean(grad, axis=-1, keepdims=True)
+    along = jnp.mean(grad * unit, axis=-1, keepdims=True)
+    return rstd * (grad - mean - unit * along)
+
+
+class Place:
+    def __init__(self):
+        dp, seq = lax.axis_index("dp"), lax.axis_index("seq")
+        self.z, self.y, self.x, self.c = dp // 2, dp % 2, seq // 2, seq % 2
+        self.shard = dp
+
+    def device(self, z=None, y=None, x=None, c=None):
+        z = self.z if z is None else z
+        y = self.y if y is None else y
+        x = self.x if x is None else x
+        c = self.c if c is None else c
+        return {"dp": z * 2 + y, "seq": x * 2 + c}
+
+    def plane(self, shift):
+        return lax.rem(self.z + shift + PLANES, PLANES)
+
+    def across_y(self):
+        return self.device(y=1 - self.y)
+
+    def across_x(self):
+        return self.device(x=1 - self.x)
+
+    def across_c(self):
+        return self.device(c=1 - self.c)
+
+    def neighbours(self):
+        planes = [self.device(z=self.plane(step)) for step in range(1, PLANES)]
+        return planes + [self.across_y(), self.across_x(), self.across_c()]
+
+    def corners(self):
+        y, x, c = 1 - self.y, 1 - self.x, 1 - self.c
+        return [
+            self.device(x=x, c=c), self.device(y=y, c=c),
+            self.device(y=y, x=x), self.device(y=y, x=x, c=c),
+        ]
+
+    def in_plane(self):
+        return (self.y * 2 + self.x) * 2 + self.c
+
+
+def greet(place, corners=False):
+    barrier = pltpu.get_barrier_semaphore()
+    peers = place.neighbours() + (place.corners() if corners else [])
+    for peer in peers:
+        pl.semaphore_signal(barrier, inc=1, device_id=peer, device_id_type=MESH)
+    pl.semaphore_wait(barrier, len(peers))
+
+
+class Engine:
+    RATES = {"x": 30e3, "y": 30e3, "z": 23e3, "c": 200e3}
+
+    def __init__(self, pace=1.0):
+        self.now, self.free, self.pace = 0.0, dict.fromkeys(self.RATES, 0.0), pace
+        self.eta, self.tasks, self.done = {}, [], set()
+
+    def sent(self, key, link, size):
+        self.now += 0.04
+        start = max(self.now, self.free[link])
+        self.free[link] = start + size / (self.pace * self.RATES[link])
+        self.eta[key] = self.free[link] + 1.5
+
+    def add(self, needs, act, mark=None, cost=0.05):
+        self.tasks.append((needs, act, mark, cost))
+
+    def due(self, task):
+        return max((self.eta.get(key, math.inf) for key in task[0]), default=0.0)
+
+    def run(self, task):
+        self.tasks.remove(task)
+        self.now = max(self.now, self.due(task)) + task[3]
+        task[1]()
+        if task[2] is not None:
+            self.done.add(task[2])
+
+    def tick(self, cost):
+        self.now += cost
+        while self.tasks:
+            task = min(self.tasks, key=self.due)
+            if self.due(task) > self.now:
+                return
+            self.run(task)
+
+    def until(self, *marks):
+        while not self.done.issuperset(marks):
+            self.run(min(self.tasks, key=self.due))
+
+    def rest(self):
+        while self.tasks:
+            self.run(min(self.tasks, key=self.due))
+
+
+class Gather:
+    def __init__(self, place, engine, chunks, send, recv, ready):
+        self.place, self.engine, self.chunks = place, engine, chunks
+        self.send, self.recv, self.sent, self.ready = send, recv, [], ready
+        for k in range(len(chunks)):
+            self.plan(k)
+
+    def piece(self, k, z, y, x, c):
+        ref, stride, base, height, column, width = self.chunks[k]
+        row = (z * 2 + y) * stride + base + c * height
+        return ref.at[
+            pl.ds(pl.multiple_of(row, 16), height),
+            pl.ds(pl.multiple_of(column + x * width, 128), width),
+        ]
+
+    def copy(self, k, index, ref, device):
+        return pltpu.make_async_remote_copy(
+            src_ref=ref,
+            dst_ref=ref,
+            send_sem=self.send.at[k, index],
+            recv_sem=self.recv.at[k, index],
+            device_id=device,
+            device_id_type=MESH,
+        )
+
+    def push(self, k, index, ref, device, link):
+        copy = self.copy(k, index, ref, device)
+        copy.start()
+        self.sent.append(copy)
+        self.engine.sent((k, index), link, 2 * self.chunks[k][3] * self.chunks[k][5])
+
+    def pull(self, k, index, ref):
+        self.copy(k, index, ref, self.place.across_c()).wait_recv()
+
+    def twin(self, k, index, ref):
+        self.push(k, 14 + index, ref, self.place.across_c(), "c")
+
+    def begin(self, k):
+        p = self.place
+        self.ready(k)
+        own = self.piece(k, p.z, p.y, p.x, p.c)
+        for step in (1, 3, 2):
+            self.push(k, step - 1, own, p.device(z=p.plane(step)), "z")
+        self.push(k, 3, own, p.across_y(), "y")
+        other = self.piece(k, p.z, p.y, 1 - p.x, p.c)
+        self.push(k, 10, other, p.across_y(), "y")
+        self.push(k, 7, other, p.device(z=p.plane(1)), "z")
+
+    def from_plane(self, k, step):
+        p = self.place
+        ref = self.piece(k, p.plane(-step), p.y, p.x, p.c)
+        self.pull(k, step - 1, ref)
+        self.push(k, 3 + step, ref, p.across_y(), "y")
+        if step != 1:
+            self.push(k, 6 + step, ref, p.across_x(), "x")
+        self.twin(k, step - 1, ref)
+
+    def by_y(self, k):
+        return (1, 3) if k == 6 else ()
+
+    def from_y(self, k, step):
+        p = self.place
+        ref = self.piece(k, p.plane(-step), 1 - p.y, p.x, p.c)
+        self.pull(k, 3 + step, ref)
+        if step and step not in self.by_y(k):
+            self.push(k, 10 + step, ref, p.across_x(), "x")
+        self.twin(k, 3 + step, ref)
+
+    def from_x(self, k, step):
+        p = self.place
+        ref = self.piece(k, p.plane(-step), p.y, 1 - p.x, p.c)
+        self.pull(k, 6 + step, ref)
+        if step in self.by_y(k):
+            self.push(k, 10 + step, ref, p.across_y(), "y")
+        self.twin(k, 6 + step, ref)
+
+    def corner(self, k, step):
+        p = self.place
+        ref = self.piece(k, p.plane(-step), 1 - p.y, 1 - p.x, p.c)
+        self.pull(k, 10 + step, ref)
+        self.twin(k, 10 + step, ref)
+
+    def finish(self, k):
+        p = self.place
+        far = 1 - p.c
+        for step in range(PLANES):
+            z = p.plane(-step)
+            if step:
+                self.pull(k, 14 + step - 1, self.piece(k, z, p.y, p.x, far))
+                self.pull(k, 20 + step, self.piece(k, z, p.y, 1 - p.x, far))
+            self.pull(k, 17 + step, self.piece(k, z, 1 - p.y, p.x, far))
+            self.pull(k, 24 + step, self.piece(k, z, 1 - p.y, 1 - p.x, far))
+
+    def plan(self, k):
+        before = [(k - 2, at) for at in range(3)] if k > 1 else []
+        add = self.engine.add
+        add(before, functools.partial(self.begin, k))
+        for step in (1, 3, 2):
+            add([(k, step - 1)], functools.partial(self.from_plane, k, step))
+            add([(k, 6 + step)], functools.partial(self.from_x, k, step))
+        for step in (0, 1, 3, 2):
+            add([(k, 3 + step)], functools.partial(self.from_y, k, step))
+            add([(k, 10 + step)], functools.partial(self.corner, k, step))
+        add([(k, 14 + at) for at in range(14)], functools.partial(self.finish, k), k, 0.3)
+
+    def drain(self):
+        for copy in self.sent:
+            copy.wait_send()
+
+
+def ds(start, size, unit):
+    return pl.ds(pl.multiple_of(start, unit), size)
+
+
+def turn_over(source, target):
+    for at in range(0, source.shape[0], 256):
+        target[:, at : at + 256] = source[at : at + 256, :].T
+
+
+def block_of(b):
+    return ds((b // 6) * PIECE, PIECE, PIECE), ds(lax.rem(b, 6) * PAIR, PAIR, PAIR)
+
+
+def forward_kernel(
+    x_h, attn_h, up_h, down_h, norm_h, trig_h,
+    wqkv_o, wo_o, wup_o, wdn_o, q_o, k_o, v_o, att_o, rden_o, xhat_o, rstd_o, xt_o, att_t_o,
+    low_t_o, act_o, slope_o, state_o,
+    wqkv, wo, wup, wdn, attn_st, up_st, down_st, x_s, norm_s, trig_s, tri_s,
+    q_s, k_s, v_s, num_s, den_s, att_s, xhat_s, rstd_s, low_s, act_s, slope_a, slope_b, hid_a, hid_b,
+    x_t_s, att_t_s, low_t_s, st_own, st_twin, st_chip, st_prior,
+    load_sem, store_sem, tile_sem, g_send, g_recv, st_send, st_recv,
+):
+    place = Place()
+    shard, x, c = place.shard, place.x, place.c
+    groups = x_s.shape[0] // PIECE
+    blocks = groups * 6
+    loads = []
+    for at, (src, dst) in enumerate(
+        [
+            (attn_h, attn_st), (up_h, up_st), (down_h, down_st), (x_h, x_s), (norm_h, norm_s),
+            (trig_h.at[ds((x * 2 + c) * PIECE, PIECE, PIECE), :], trig_s),
+        ]
+    ):
+        copy = pltpu.make_async_copy(src, dst, load_sem.at[at])
+        copy.start()
+        loads.append(copy)
+    stores = []
+
+    def store(src, dst):
+        copy = pltpu.make_async_copy(src, dst, store_sem.at[len(stores)])
+        copy.start()
+        stores.append(copy)
+
+    thin, thick = attn_st.shape[0], down_st.shape[0]
+    chunks = [
+        (wqkv, thin, 0, thin // 2, D, D),
+        (wqkv, thin, 0, thin // 2, 0, D // 2),
+        (wo, thin, 0, thin // 2, 0, D // 2),
+        (wup, thin, 0, thin // 2, 0, FF // 4),
+        (wup, thin, 0, thin // 2, FF // 2, FF // 4),
+        (wdn, thick, 0, thick // 4, 0, D // 2),
+        (wdn, thick, thick // 2, thick // 4, 0, D // 2),
+    ]
+    def ready(k):
+        narrow = ds(shard * thin, thin, 32)
+        if k == 0:
+            loads[0].wait()
+            for j in range(3):
+                wqkv[narrow, j * D : (j + 1) * D] = attn_st[:, j, :].astype(bf16)
+        elif k == 2:
+            wo[narrow, :] = attn_st[:, 3, :].astype(bf16)
+        elif k == 3:
+            loads[1].wait()
+            wup[narrow, :] = up_st[...].astype(bf16)
+        elif k == 5:
+            loads[2].wait()
+            wdn[ds(shard * thick, thick, 128), :] = down_st[...].astype(bf16)
+
+    engine = Engine()
+    gather = Gather(place, engine, chunks, g_send, g_recv, ready)
+    greet(place)
+    engine.tick(0.0)
+    fill_triangles(tri_s)
+    for copy in loads[3:]:
+        copy.wait()
+    turn_over(x_s, x_t_s)
+    store(x_t_s, xt_o)
+    engine.tick(3.0)
+    engine.until(0)
+
+    hidden = (hid_a, hid_b)
+
+    def chain(products, finish, cost):
+        hidden[0][...] = products[0]()
+        for t in range(len(products)):
+            if t + 1 < len(products):
+                hidden[(t + 1) % 2][...] = products[t + 1]()
+            finish(t, hidden[t % 2])
+            engine.tick(cost)
+
+    def project(parts):
+        tiles = [(target, column, t, soft) for target, column, soft in parts for t in range(3)]
+
+        def product(target, column, t, soft):
+            return dot(x_s[...], wqkv[:, column + 256 * t : column + 256 * t + 256])
+
+        def finish(at, pre):
+            target, _, t, soft = tiles[at]
+            pre = pre[...]
+            if soft:
+                pre = jnp.maximum(pre, 0.0) + jnp.log1p(jnp.exp(-jnp.abs(pre)))
+            target[:, 256 * t : 256 * t + 256] = pre.astype(bf16)
+
+        chain([functools.partial(product, *tile) for tile in tiles], finish, 0.7)
+
+    project([(k_s, D, True), (v_s, 2 * D, False)])
+
+    def local(b, carry):
+        rows, cols = ds((b // 6) * PIECE, PIECE, PIECE), ds(lax.rem(b, 6) * PAIR, PAIR, PAIR)
+        keys = turned(k_s[rows, cols], trig_s[...])
+        state = dot_tn(keys, v_s[rows, cols])
+        totals = dot(jnp.ones((16, PIECE), bf16), keys)
+        st_own[b] = squeeze_state(state, totals).astype(bf16)
+        return carry
+
+    for part in range(0, blocks, 4):
+        lax.fori_loop(part, part + 4, local, 0)
+        engine.tick(1.4)
+    state = StateSum(place, engine, st_send, st_recv, st_own, st_twin, st_chip, st_prior, False)
+    engine.tick(0.0)
+    engine.until(1)
+    project([(q_s, 0, True)])
+    store(wqkv, wqkv_o)
+    store(q_s, q_o)
+    store(k_s, k_o)
+    store(v_s, v_o)
+
+    def intra(i, carry):
+        spots = [block_of(2 * i), block_of(2 * i + 1)]
+        taken = [(q_s[at], k_s[at], v_s[at]) for at in spots]
+        outs = [
+            causal_product(
+                turned(q, trig_s[...]), turned(k, trig_s[...]), with_ones(v), tri_s
+            )
+            for q, k, v in taken
+        ]
+        for at, out in zip(spots, outs):
+            num_s[at] = out[:, :PAIR]
+            den_s[at] = out[:, PAIR:]
+        return carry
+
+    for part in range(blocks // 2):
+        lax.fori_loop(part, part + 1, intra, 0)
+        engine.tick(1.6)
+    engine.until("state")
+
+    def inter(i, carry):
+        spots = [block_of(2 * i), block_of(2 * i + 1)]
+        states = [state.total(2 * i + at).astype(bf16) for at in range(2)]
+        taken = [(q_s[at], num_s[at], den_s[at]) for at in spots]
+        outs = []
+        for (q, num, den), packed in zip(taken, states):
+            more = dot(turned(q, trig_s[...]), spread_state(packed))
+            recip = 1.0 / (den + more[:, PAIR:])
+            outs.append((((num + more[:, :PAIR]) * recip).astype(bf16), recip))
+        for at, (attended, recip) in zip(spots, outs):
+            att_s[at] = attended
+            den_s[at] = recip
+        for at, packed in enumerate(states):
+            st_chip[2 * i + at] = packed
+        return carry
+
+    for part in range(0, blocks // 2, 2):
+        lax.fori_loop(part, part + 2, inter, 0)
+        engine.tick(1.6)
+    store(att_s, att_o)
+    store(den_s, rden_o)
+    turn_over(att_s, att_t_s)
+    store(att_t_s, att_t_o)
+    store(st_chip, state_o)
+    engine.tick(1.0)
+    engine.until(2)
+    store(wo, wo_o)
+
+    gain_one, bias_one = norm_s[0:1, :], norm_s[1:2, :]
+    tile = 256
+
+    def join(t, carry):
+        cols = ds(t * tile, tile, tile)
+        xhat_s[:, cols] = x_s[:, cols].astype(f32) + dot(att_s[...], wo[:, cols])
+        return carry
+
+    def join_norm(t, carry):
+        rows = ds(t * tile, tile, tile)
+        unit, rstd = normed(xhat_s[rows, :])
+        xhat_s[rows, :] = unit
+        rstd_s[rows, :] = jnp.broadcast_to(rstd, (tile, 128))
+        low_s[rows, :] = (unit * gain_one + bias_one).astype(bf16)
+        return carry
+
+    for t in range(D // tile):
+        lax.fori_loop(t, t + 1, join, 0)
+        engine.tick(0.7)
+    for part in range(x_s.shape[0] // tile):
+        lax.fori_loop(part, part + 1, join_norm, 0)
+        engine.tick(0.4)
+    store(xhat_s, xhat_o)
+    store(rstd_s, rstd_o)
+    turn_over(low_s, low_t_s)
+    store(low_t_s, low_t_o)
+    engine.tick(1.0)
+    engine.until(3)
+
+    slopes, scale = (slope_a, slope_b), math.sqrt(2.0 / math.pi)
+
+    def slope_copy(t):
+        return pltpu.make_async_copy(
+            slopes[t % 2], slope_o.at[:, 256 * t : 256 * t + 256], tile_sem.at[t % 2]
+        )
+
+    def expand(t, value):
+        if t >= 2:
+            slope_copy(t - 2).wait()
+        value = value[...]
+        squared = value * value
+        curve = jnp.tanh(value * (scale + (scale * 0.044715) * squared))
+        half = 0.5 + 0.5 * curve
+        active = value * half
+        slope = half + active * (1.0 - curve) * (scale + (3.0 * scale * 0.044715) * squared)
+        act_s[:, 256 * t : 256 * t + 256] = active.astype(bf16)
+        slopes[t % 2][...] = slope.astype(bf16)
+        slope_copy(t).start()
+
+    def raised(t):
+        if t == 6:
+            engine.until(4)
+            store(wup, wup_o)
+        return dot(low_s[...], wup[:, 256 * t : 256 * t + 256])
+
+    chain([functools.partial(raised, t) for t in range(FF // 256)], expand, 1.1)
+    store(act_s, act_o)
+    engine.until(5, 6)
+    store(wdn, wdn_o)
+    for copy in stores + [slope_copy(10), slope_copy(11)]:
+        copy.wait()
+    gather.drain()
+    state.drain()
+
+
+def forward_call(tokens, attn_master, up_master, down_master, norm_params, seq_count):
+    rows = tokens.shape[0]
+    blocks = rows // PIECE * 6
+    thin, thick = attn_master.shape[0], down_master.shape[0]
+    trig = turning_table(seq_count)
+    shapes = dict(
+        wqkv=((D, 3 * D), bf16), wo=((D, D), bf16), wup=((D, FF), bf16), wdn=((FF, D), bf16),
+        q=((rows, D), bf16), k=((rows, D), bf16), v=((rows, D), bf16), att=((rows, D), bf16),
+        rden=((rows, D), f32), xhat=((rows, D), f32), rstd=((rows, 128), f32),
+        x_t=((D, rows), bf16), att_t=((D, rows), bf16), low_t=((D, rows), bf16),
+        act=((rows, FF), bf16), slope=((rows, FF), bf16), state=((blocks, 144, PAIR), bf16),
+    )
+    out_shape = [jax.ShapeDtypeStruct(s, d) for s, d in shapes.values()]
+    hbm = pl.BlockSpec(memory_space=pl.ANY)
+    scratch = [
+        pltpu.VMEM((D, 3 * D), bf16), pltpu.VMEM((D, D), bf16),
+        pltpu.VMEM((D, FF), bf16), pltpu.VMEM((FF, D), bf16),
+        pltpu.VMEM((thin, 4, D), f32), pltpu.VMEM((thin, FF), f32), pltpu.VMEM((thick, D), f32),
+        pltpu.VMEM((rows, D), bf16), pltpu.VMEM((4, D), f32),
+        pltpu.VMEM((PIECE, 2 * PAIR), f32), pltpu.VMEM((PIECE, PIECE // 2), bf16),
+        pltpu.VMEM((rows, D), bf16), pltpu.VMEM((rows, D), bf16), pltpu.VMEM((rows, D), bf16),
+        pltpu.VMEM((rows, D), f32), pltpu.VMEM((rows, D), f32), pltpu.VMEM((rows, D), bf16),
+        pltpu.VMEM((rows, D), f32), pltpu.VMEM((rows, 128), f32), pltpu.VMEM((rows, D), bf16),
+        pltpu.VMEM((rows, FF), bf16), pltpu.VMEM((rows, 256), bf16),
+        pltpu.VMEM((rows, 256), bf16), pltpu.VMEM((rows, 256), f32),
+        pltpu.VMEM((rows, 256), f32),
+        pltpu.VMEM((D, rows), bf16), pltpu.VMEM((D, rows), bf16), pltpu.VMEM((D, rows), bf16),
+        pltpu.VMEM((blocks, 144, PAIR), bf16), pltpu.VMEM((blocks, 144, PAIR), bf16),
+        pltpu.VMEM((blocks, 144, PAIR), bf16), pltpu.VMEM((blocks, 144, PAIR), bf16),
+        pltpu.SemaphoreType.DMA((8,)), pltpu.SemaphoreType.DMA((21,)),
+        pltpu.SemaphoreType.DMA((2,)),
+        pltpu.SemaphoreType.DMA((7, 28)), pltpu.SemaphoreType.DMA((7, 28)),
+        pltpu.SemaphoreType.DMA((3,)), pltpu.SemaphoreType.DMA((3,)),
+    ]
+    return dict(
+        zip(
+            shapes,
+            pl.pallas_call(
+                forward_kernel,
+                out_shape=out_shape,
+                in_specs=[hbm] * 6,
+                out_specs=[hbm] * len(out_shape),
+                scratch_shapes=scratch,
+                compiler_params=pltpu.CompilerParams(
+                    collective_id=0, has_side_effects=True, vmem_limit_bytes=VMEM_BYTES
+                ),
+                name="gather_forward",
+            )(
+                tokens, attn_master, up_master, down_master, norm_params,
+                trig,
+            ),
+        )
+    )
+
+
+def second_norm_kernel(
+    act, wdn, xhat, cot, norm, out_o, gb_o, gb_t_o, gr2_o, sums_o, sum_s
+):
+    rows = act.shape[0]
+    for column in range(0, D, 256):
+        cols = slice(column, column + 256)
+        sum_s[:, cols] = dot(act[...], wdn[:, cols])
+
+    @pl.when(pl.program_id(0) == 0)
+    def _():
+        sums_o[...] = jnp.zeros_like(sums_o)
+
+    def body(t, carry):
+        span = ds(t * 256, 256, 256)
+        first = xhat[span, :] * norm[0:1, :] + norm[1:2, :]
+        unit, rstd = normed(first + sum_s[span, :])
+        out_o[span, :] = (unit * norm[2:3, :] + norm[3:4, :]).astype(bf16)
+        grad = cot[span, :].astype(f32)
+        sums_o[0:1, :] += jnp.sum(grad * unit, axis=0, keepdims=True)
+        sums_o[1:2, :] += jnp.sum(grad, axis=0, keepdims=True)
+        grad = norm_back(grad * norm[2:3, :], unit, rstd)
+        gr2_o[span, :] = grad
+        low = grad.astype(bf16)
+        gb_o[span, :] = low
+        gb_t_o[:, span] = low.T
+        return carry
+
+    lax.fori_loop(0, rows // 256, body, 0)
+
+
+def second_norm(s, cotangent, norm_params):
+    rows = cotangent.shape[0]
+    tile = rows // 2
+    by_rows = lambda width: pl.BlockSpec((tile, width), lambda t: (t, 0))
+    whole = lambda height, width: pl.BlockSpec((height, width), lambda t: (0, 0))
+    outs = pl.pallas_call(
+        second_norm_kernel,
+        grid=(rows // tile,),
+        in_specs=[by_rows(FF), whole(FF, D), by_rows(D), by_rows(D), whole(4, D)],
+        out_specs=[
+            by_rows(D), by_rows(D), pl.BlockSpec((D, tile), lambda t: (0, t)), by_rows(D),
+            whole(8, D),
+        ],
+        out_shape=[
+            jax.ShapeDtypeStruct((rows, D), bf16), jax.ShapeDtypeStruct((rows, D), bf16),
+            jax.ShapeDtypeStruct((D, rows), bf16), jax.ShapeDtypeStruct((rows, D), f32),
+            jax.ShapeDtypeStruct((8, D), f32),
+        ],
+        scratch_shapes=[pltpu.VMEM((tile, D), f32)],
+        compiler_params=pltpu.CompilerParams(vmem_limit_bytes=VMEM_BYTES),
+        name="second_norm",
+    )(s["act"], s["wdn"], s["xhat"], cotangent, norm_params)
+    return dict(zip(("out", "gb", "gb_t", "gr2", "sums"), outs))
+
+
+def input_kernel(gp, w, part, out):
+    for column in range(0, D, 256):
+        cols = slice(column, column + 256)
+        out[:, cols] = part[:, cols] + dot_nt(gp[...], w[cols, :])
+
+
+def input_call(gp, w, part):
+    rows = part.shape[0]
+    tile = rows // 2
+    by_rows = lambda width: pl.BlockSpec((tile, width), lambda t: (t, 0))
+    return pl.pallas_call(
+        input_kernel,
+        grid=(rows // tile,),
+        in_specs=[by_rows(3 * D), pl.BlockSpec((D, 3 * D), lambda t: (0, 0)), by_rows(D)],
+        out_specs=by_rows(D),
+        out_shape=jax.ShapeDtypeStruct((rows, D), f32),
+        compiler_params=pltpu.CompilerParams(vmem_limit_bytes=VMEM_BYTES),
+        name="input_gradient",
+    )(gp, w, part)
+
+
+def turning_table(seq_count):
+    length = seq_count * PIECE
+    angle = math.pi / 2 * np.arange(length, dtype=np.float64) / length
+    trig = np.repeat(np.stack([np.cos(angle), np.sin(angle)], axis=1), PAIR, axis=1)
+    return jnp.asarray(trig, f32)
+
+
+class Share:
+    def __init__(self, grad, first, units, column, width, by_units, early, bufs, out):
+        self.grad, self.first, self.units = grad, first, units
+        self.column, self.width, self.by_units, self.early = column, width, by_units, early
+        self.count = units // 2 if by_units else units
+        self.half = width if by_units else width // 2
+        self.twin, self.from_x, self.from_y, self.via_x, self.via_y, self.planes, self.final = bufs
+        self.out = out
+
+    def side(self, x):
+        if self.by_units:
+            return x * self.count, slice(0, self.width)
+        return 0, ds(x * self.half, self.half, 128)
+
+    def part(self, x):
+        first, lanes = self.side(x)
+        return pl.ds(first, self.count), lanes
+
+
+def add_into(target, at, other, there, more=None, where=None):
+    total = target[at].astype(f32) + other[there].astype(f32)
+    if more is not None:
+        total = total + more[where].astype(f32)
+    target[at] = total.astype(bf16)
+
+
+class Reduce:
+    def __init__(self, place, engine, send, recv, store_sem, squares):
+        self.place, self.engine, self.send, self.recv = place, engine, send, recv
+        self.store_sem, self.squares = store_sem, squares
+        self.sent, self.stored, self.count = [], [], 0
+
+    def copy(self, k, index, src, dst, device):
+        return pltpu.make_async_remote_copy(
+            src_ref=src, dst_ref=dst, send_sem=self.send.at[k, index],
+            recv_sem=self.recv.at[k, index], device_id=device, device_id_type=MESH,
+        )
+
+    def push(self, k, index, src, dst, device, link):
+        copy = self.copy(k, index, src, dst, device)
+        copy.start()
+        self.sent.append((k, index, copy))
+        self.engine.sent(("part", k, index), link, 2 * math.prod(dst.shape))
+
+    def settle(self, parts):
+        for k, index, copy in list(self.sent):
+            if k in parts and index == 0:
+                copy.wait_send()
+                self.sent.remove((k, index, copy))
+
+    def pull(self, k, index, dst):
+        self.copy(k, index, dst, dst, self.place.across_c()).wait_recv()
+
+    def launch(self, share):
+        k = self.count
+        self.count += 1
+        src = share.grad.at[
+            share.first : share.first + share.units, :, :, 1 - self.place.c, :,
+            share.column : share.column + share.width,
+        ]
+        self.push(k, 0, src, share.twin, self.place.across_c(), "c")
+        for needs, act, mark, cost in [
+            ((0,), self.fold_core, "core", 0.8),
+            ((1, 2), self.fold_corner, None, 0.3),
+            ((3, 4, 5, 6), self.fold_square, None, 0.4),
+            ((7, 8, 9), self.fold_planes, "sum", 0.3),
+            ((10,), self.share_x, None, 0.05),
+            ((11,), self.share_c, "whole", 0.05),
+        ]:
+            keys = [("part", k, at) for at in needs]
+            self.engine.add(keys, functools.partial(act, k, share), (mark, k), cost)
+
+    def fold_core(self, k, s):
+        p = self.place
+        self.pull(k, 0, s.twin)
+
+        def body(i, carry):
+            u, z = i // PLANES, lax.rem(i, PLANES)
+            for y in range(2):
+                own = s.grad[s.first + u, z, y, p.c, :, s.column : s.column + s.width]
+                total = s.twin[u, z, y].astype(f32) + own.astype(f32)
+                s.twin[u, z, y] = total.astype(bf16)
+            return carry
+
+        lax.fori_loop(0, PLANES * s.units, body, 0)
+        e, oy, t = s.early, 1 - p.y, s.twin
+        (mine, near), (theirs, far) = s.part(p.x), s.part(1 - p.x)
+        self.push(k, 1, t.at[theirs, 0:e, oy, :, far], s.via_x, p.across_x(), "x")
+        self.push(k, 2, t.at[theirs, e:PLANES, oy, :, far], s.via_y, p.across_y(), "y")
+        self.push(
+            k, 3, t.at[theirs, 0:e, p.y, :, far], s.from_x.at[:, 0:e], p.across_x(), "x"
+        )
+        self.push(
+            k, 4, t.at[mine, e:PLANES, oy, :, near], s.from_y.at[:, e:PLANES], p.across_y(), "y"
+        )
+
+    def fold_corner(self, k, s):
+        p, e, t, oy = self.place, s.early, s.twin, 1 - self.place.y
+        (mine, near), (theirs, far) = s.part(p.x), s.part(1 - p.x)
+        self.pull(k, 1, s.via_x)
+
+        def from_x(u, carry):
+            for z in range(e):
+                add_into(t, (s.side(p.x)[0] + u, z, oy, slice(None), near), s.via_x, (u, z))
+            return carry
+
+        lax.fori_loop(0, s.count, from_x, 0)
+        self.push(k, 5, t.at[mine, 0:e, oy, :, near], s.from_y.at[:, 0:e], p.across_y(), "y")
+        self.pull(k, 2, s.via_y)
+
+        def from_y(u, carry):
+            for z in range(e, PLANES):
+                at = (s.side(1 - p.x)[0] + u, z, p.y, slice(None), far)
+                add_into(t, at, s.via_y, (u, z - e))
+            return carry
+
+        lax.fori_loop(0, s.count, from_y, 0)
+        self.push(
+            k, 6, t.at[theirs, e:PLANES, p.y, :, far], s.from_x.at[:, e:PLANES], p.across_x(), "x"
+        )
+
+    def fold_square(self, k, s):
+        p, e, t = self.place, s.early, s.twin
+        mine, near = s.part(p.x)
+        self.pull(k, 3, s.from_x.at[:, 0:e])
+        self.pull(k, 4, s.from_y.at[:, e:PLANES])
+        self.pull(k, 5, s.from_y.at[:, 0:e])
+        self.pull(k, 6, s.from_x.at[:, e:PLANES])
+
+        def body(i, carry):
+            u, z = i // PLANES, lax.rem(i, PLANES)
+            at = (s.side(p.x)[0] + u, z, p.y, slice(None), near)
+            add_into(t, at, s.from_x, (u, z), s.from_y, (u, z))
+            return carry
+
+        lax.fori_loop(0, PLANES * s.count, body, 0)
+        for step in (1, 3, 2):
+            z = p.plane(step)
+            self.push(
+                k, 6 + step, t.at[mine, z, p.y, :, near], s.planes.at[:, step - 1],
+                p.device(z=z), "z",
+            )
+
+    def fold_planes(self, k, s):
+        p = self.place
+        mine, near = s.part(p.x)
+        for step in (1, 3, 2):
+            self.pull(k, 6 + step, s.planes.at[:, step - 1])
+
+        def body(u, carry):
+            at = s.side(p.x)[0] + u
+            total = s.twin[at, p.z, p.y, :, near].astype(f32)
+            for step in range(3):
+                total = total + s.planes[u, step].astype(f32)
+            total = total.astype(bf16)
+            s.final[at, p.c, :, near] = total
+            wide = total.astype(f32)
+            for lane in range(0, s.half, 128):
+                part = wide[:, lane : lane + 128]
+                self.squares[...] += jnp.sum((part * part).reshape(-1, 8, 128), axis=0)
+            return carry
+
+        lax.fori_loop(0, s.count, body, 0)
+        piece = s.final.at[mine, p.c, :, near]
+        self.push(k, 10, piece, piece, p.across_x(), "x")
+
+    def share_x(self, k, s):
+        p = self.place
+        theirs, far = s.part(1 - p.x)
+        self.pull(k, 10, s.final.at[theirs, p.c, :, far])
+        half = s.final.at[:, p.c]
+        self.push(k, 11, half, half, p.across_c(), "c")
+
+    def share_c(self, k, s):
+        self.pull(k, 11, s.final.at[:, 1 - self.place.c])
+        copy = pltpu.make_async_copy(s.final, s.out, self.store_sem.at[k])
+        copy.start()
+        self.stored.append(copy)
+
+    def drain(self):
+        for _, _, copy in self.sent:
+            copy.wait_send()
+        for copy in self.stored:
+            copy.wait()
+
+
+class Total:
+    def __init__(self, place, engine, name, value, near, planes, send, recv):
+        self.place, self.engine, self.name = place, engine, name
+        self.value, self.near, self.planes = value, near, planes
+        self.send, self.recv, self.sent = send, recv, []
+        y, x, c = 1 - place.y, 1 - place.x, 1 - place.c
+        peers = [place.across_c(), place.across_x(), place.across_y()] + place.corners()
+        flips = [(0, 0, 1), (0, 1, 0), (1, 0, 0), (0, 1, 1), (1, 0, 1), (1, 1, 0), (1, 1, 1)]
+        self.slots = [
+            ((y if flip[0] else place.y) * 2 + (x if flip[1] else place.x)) * 2
+            + (c if flip[2] else place.c)
+            for flip in flips
+        ]
+        own = near.at[place.in_plane()]
+        near[place.in_plane()] = value[...]
+        for at, peer in enumerate(peers):
+            self.push(at, own, peer, "cxyxyxy"[at])
+        engine.add([(name, at) for at in range(7)], self.across)
+
+    def copy(self, index, ref, device):
+        return pltpu.make_async_remote_copy(
+            src_ref=ref, dst_ref=ref, send_sem=self.send.at[index],
+            recv_sem=self.recv.at[index], device_id=device, device_id_type=MESH,
+        )
+
+    def push(self, index, ref, device, link):
+        copy = self.copy(index, ref, device)
+        copy.start()
+        self.sent.append(copy)
+        self.engine.sent((self.name, index), link, 4 * math.prod(ref.shape))
+
+    def across(self):
+        p = self.place
+        for at, slot in enumerate(self.slots):
+            self.copy(at, self.near.at[slot], p.across_c()).wait_recv()
+        total = self.near[0]
+        for at in range(1, 8):
+            total = total + self.near[at]
+        self.planes[p.z] = total
+        for step in (1, 3, 2):
+            self.push(6 + step, self.planes.at[p.z], p.device(z=p.plane(step)), "z")
+        self.engine.add([(self.name, at) for at in (7, 8, 9)], self.end, self.name)
+
+    def end(self):
+        for step in (1, 3, 2):
+            own = self.planes.at[self.place.plane(-step)]
+            self.copy(6 + step, own, self.place.across_c()).wait_recv()
+        self.value[...] = (self.planes[0] + self.planes[1]) + (self.planes[2] + self.planes[3])
+
+    def drain(self):
+        for copy in self.sent:
+            copy.wait_send()
+
+
+class StateSum:
+    def __init__(self, place, engine, send, recv, own, twin, chip, prior, late):
+        self.x, self.c, self.engine = place.x, place.c, engine
+        self.own, self.twin, self.chip, self.prior = own, twin, chip, prior
+        self.giver, self.taker = (1, 0) if late else (0, 1)
+        half = own.shape[0] // 2
+        self.size = math.prod(own.shape)
+        mine, other = ds(place.c * half, half, 1), ds((1 - place.c) * half, half, 1)
+
+        def copy(index, src, dst, device):
+            return pltpu.make_async_remote_copy(
+                src_ref=src, dst_ref=dst, send_sem=send.at[index], recv_sem=recv.at[index],
+                device_id=device, device_id_type=MESH,
+            )
+
+        self.swap = copy(0, own, twin, place.across_c())
+        self.over = copy(1, chip.at[mine], prior.at[mine], place.across_x())
+        self.pass_on = copy(2, prior.at[mine], prior.at[mine], place.across_c())
+        self.taken = copy(2, prior.at[other], prior.at[other], place.across_c())
+        self.swap.start()
+        engine.sent("swap", "c", 2 * self.size)
+        engine.add(["swap"], self.join, None, 0.5)
+        engine.add(["over"], self.forward)
+        engine.add(["pass"], self.end, "state")
+
+    def join(self):
+        self.swap.wait_recv()
+        self.chip[...] = (self.own[...].astype(f32) + self.twin[...].astype(f32)).astype(bf16)
+
+        @pl.when(self.x == self.giver)
+        def _():
+            self.over.start()
+
+        self.engine.sent("over", "x", self.size)
+
+    def forward(self):
+        @pl.when(self.x == self.taker)
+        def _():
+            self.over.wait_recv()
+            self.pass_on.start()
+
+        self.engine.sent("pass", "c", self.size)
+
+    def end(self):
+        @pl.when(self.x == self.taker)
+        def _():
+            self.taken.wait_recv()
+
+        @pl.when(self.x == self.giver)
+        def _():
+            self.over.wait_send()
+
+    def drain(self):
+        self.swap.wait_send()
+
+        @pl.when(self.x == self.taker)
+        def _():
+            self.pass_on.wait_send()
+
+    def total(self, b):
+        far = jnp.where(self.x == self.taker, self.prior[b].astype(f32), 0.0)
+        return far + jnp.where(self.c == self.taker, self.twin[b].astype(f32), 0.0)
+
+
+def lane_in_head(shape):
+    return lax.broadcasted_iota(jnp.int32, shape, 1) & (HEAD - 1)
+
+
+def backward_kernel(
+    wo_h, wup_h, q_h, k_h, v_h, att_h, rden_h, xhat_h, rstd_h, x_t_h, att_t_h,
+    low_t_h, act_h, slope_h, gb_h, gb_t_h, gr2_h, state_h, sums_h, wdn_h, norm_h, trig_h,
+    gp_o, one_o, attn_o, up_o, down_o, norm_o, square_o,
+    wup, acts, slope, gr2, gb, left, wide, rstd, ga_s, gd_s, gu_s,
+    norm_s, trig_s, tri_s, state_s, st_own, st_twin, st_chip, st_prior,
+    norm_v, norm_w, norm_z, sq_v, sq_w, sq_z,
+    *rest,
+):
+    bufs = rest[: 7 * SHARES]
+    load_sem, store_sem, r_send, r_recv, s_send, s_recv = rest[7 * SHARES : 7 * SHARES + 6]
+    t_send, t_recv, u_send, u_recv = rest[7 * SHARES + 6 :]
+    place = Place()
+    rows_all = gr2.shape[0]
+    blocks = state_s.shape[0]
+    tile = 256
+    count = [0]
+
+    def load(src, dst):
+        copy = pltpu.make_async_copy(src, dst, load_sem.at[count[0]])
+        count[0] += 1
+        copy.start()
+        return copy
+
+    def wait(copies):
+        for copy in copies:
+            copy.wait()
+
+    first_in = [load(gb_t_h, wup.at[:, 0:rows_all])]
+    act_in = [load(act_h.at[:, D * z : D * z + D], acts.at[:, D * z : D * z + D]) for z in range(4)]
+    next_in = [load(gb_h, gb), load(wdn_h, ga_s), load(slope_h, slope), load(low_t_h, left)]
+    mid_in = [
+        load(gr2_h, gr2), load(xhat_h, wide), load(rstd_h, rstd), load(norm_h, norm_s),
+        load(sums_h, norm_v),
+    ]
+    late_in = [
+        load(state_h, state_s),
+        load(trig_h.at[ds((place.x * 2 + place.c) * PIECE, PIECE, PIECE), :], trig_s),
+    ]
+    sq_v[...] = jnp.zeros_like(sq_v)
+    fill_triangles(tri_s)
+    engine = Engine(0.75)
+    reduce = Reduce(place, engine, r_send, r_recv, store_sem, sq_v)
+    shares = []
+    for at, (kind, first, units, column, width, by_units, early) in enumerate(share_plan()):
+        grad, out = {"down": (gd_s, down_o), "up": (gu_s, up_o), "attn": (ga_s, attn_o)}[kind]
+        cut = out.at[first : first + units, :, :, column : column + width]
+        mine = bufs[7 * at : 7 * at + 7]
+        shares.append(Share(grad, first, units, column, width, by_units, early, mine, cut))
+    shares = iter(shares)
+    greet(place, corners=True)
+    wait(first_in)
+
+    for t in range(3):
+        for z in range(PLANES):
+            if t == 0:
+                act_in[z].wait()
+            starts = [D * z + 384 * y + 128 * t for y in range(2)]
+            pair = [acts[:, start : start + 128] for start in starts]
+            part = dot(wup[:, 0:rows_all], jnp.concatenate(pair, axis=1)).astype(bf16)
+            for y in range(2):
+                own = part[:, 128 * y : 128 * y + 128].reshape(8, 2, 48, 128)
+                gd_s[:, z, y, :, :, 128 * t : 128 * t + 128] = own
+            engine.tick(0.6)
+        reduce.launch(next(shares))
+
+    mid_in.append(load(wup_h, wup))
+    for at, src in enumerate((q_h, k_h, v_h, att_h)):
+        late_in.append(load(src, acts.at[:, D * at : D * at + D]))
+    wait(next_in)
+    for at in range(12):
+        cols = slice(256 * at, 256 * at + 256)
+        down_rows = ga_s[at // 3].reshape(D, D)[256 * (at % 3) : 256 * (at % 3) + 256]
+        for part in range(0, rows_all, PIECE):
+            span = slice(part, part + PIECE)
+            grad = dot_nt(gb[span, :], down_rows) * slope[span, cols].astype(f32)
+            slope[span, cols] = grad.astype(bf16)
+        up = dot(left[...], slope[:, cols]).astype(bf16)
+        gu_s[0, :, :, :, :, cols] = up.reshape(PLANES, 2, 2, 48, tile)
+        engine.tick(1.4)
+        if at % 4 == 3:
+            reduce.launch(next(shares))
+    att_t_in = load(att_t_h, left)
+    wait(mid_in)
+    gain_one = norm_s[0:1, :]
+    norm_v[2:4, :] = norm_v[0:2, :]
+    norm_v[0:2, :] = jnp.zeros((2, D), f32)
+
+    def first_back(t, carry):
+        cols = ds(t * tile, tile, tile)
+        for part in range(0, rows_all, PIECE):
+            span = slice(part, part + PIECE)
+            gr2[span, cols] += dot_nt(slope[span, :], wup[cols, :])
+        return carry
+
+    def norm_part(t, carry):
+        rows = ds(t * 128, 128, 128)
+        unit, grad = wide[rows, :], gr2[rows, :]
+        norm_v[0:1, :] += jnp.sum(grad * unit, axis=0, keepdims=True)
+        norm_v[1:2, :] += jnp.sum(grad, axis=0, keepdims=True)
+        grad = norm_back(grad * gain_one, unit, rstd[rows, 0:1])
+        gr2[rows, :] = grad
+        gb[rows, :] = grad.astype(bf16)
+        return carry
+
+    for part in range(3):
+        lax.fori_loop(part, part + 1, first_back, 0)
+        engine.tick(2.2)
+    wo_in = load(wo_h, wup.at[:, 3 * D : 4 * D])
+    for part in range(0, rows_all // 128, 4):
+        lax.fori_loop(part, part + 4, norm_part, 0)
+        engine.tick(0.8)
+    norms = Total(place, engine, "norms", norm_v, norm_w, norm_z, t_send, t_recv)
+    rden_in = load(rden_h, wide)
+    att_t_in.wait()
+
+    def outer(unit, column, grad):
+        part = dot(left[...], grad).astype(bf16)
+        part = part.reshape(PLANES, 2, 2, 48, 256)
+        ga_s[unit, :, :, :, :, column : column + 256] = part
+        engine.tick(0.6)
+
+    for t in range(3):
+        outer(3, 256 * t, gb[:, 256 * t : 256 * t + 256])
+    reduce.launch(next(shares))
+    x_t_in = load(x_t_h, left)
+    wait(late_in)
+    rden_in.wait()
+    wo_in.wait()
+    square = (2 * PAIR, PAIR)
+    row_half = (lax.broadcasted_iota(jnp.int32, square, 0) & (PAIR - 1)) < HEAD
+    by_head = (row_half == first_half(square)).astype(f32).astype(bf16)
+
+    def split(i, carry):
+        g, t = i // 3, lax.rem(i, 3)
+        rows = ds(g * PIECE, PIECE, PIECE)
+        grad = dot_nt(gb[rows, :], wup[ds(t * tile, tile, tile), 3 * D : 4 * D])
+        for pair in range(2):
+            base = t * tile + pair * PAIR
+            cols, num_cols = ds(base, PAIR, PAIR), ds(3 * D + base, PAIR, PAIR)
+            mine = grad[:, pair * PAIR : pair * PAIR + PAIR]
+            recip = wide[rows, cols]
+            along = mine * acts[rows, num_cols].astype(f32)
+            high = along.astype(bf16)
+            rest = (along - high.astype(f32)).astype(bf16)
+            gden = -dot(jnp.concatenate([high, rest], axis=1), by_head) * recip
+            high = gden.astype(bf16).astype(f32)
+            lane = lane_in_head(gden.shape)
+            both = jnp.where(lane == 0, high, jnp.where(lane == 1, gden - high, 0.0))
+            acts[rows, num_cols] = both.astype(bf16)
+            slope[rows, num_cols] = (mine * recip).astype(bf16)
+        return carry
+
+    for part in range(0, blocks // 2, 2):
+        lax.fori_loop(part, part + 2, split, 0)
+        engine.tick(1.6)
+
+    def column_of(b, group):
+        return ds(group * D + lax.rem(b, 6) * PAIR, PAIR, PAIR)
+
+    def local(b, carry):
+        rows, cols = block_of(b)
+        queries = turned(acts[rows, cols], trig_s[...])
+        state = dot_tn(queries, slope[rows, column_of(b, 3)])
+        cross = dot_tn(acts[rows, column_of(b, 3)], queries)
+        shape = (PAIR, 2 * PAIR)
+        kept = jnp.where(top_half(shape) == pair_mask(shape), cross, 0.0)
+        totals = jnp.broadcast_to(jnp.sum(kept, axis=0, keepdims=True), (16, 2 * PAIR))
+        st_own[b] = squeeze_state(state, totals).astype(bf16)
+        return carry
+
+    for part in range(0, blocks, 4):
+        lax.fori_loop(part, part + 4, local, 0)
+        engine.tick(1.5)
+    state = StateSum(place, engine, s_send, s_recv, st_own, st_twin, st_chip, st_prior, True)
+
+    def soft_slope(feature):
+        return 1.0 - jnp.exp(-feature.astype(f32))
+
+    def take(b):
+        rows, cols = block_of(b)
+        num, den = slope[rows, column_of(b, 3)], acts[rows, column_of(b, 3)]
+        q, k, v = (acts[rows, column_of(b, group)] for group in range(3))
+        return jnp.concatenate([num, den], axis=1), num, q, k, v
+
+    def query_grad(i, carry):
+        marks = [2 * i, 2 * i + 1]
+        taken = [take(b) + (state_s[b],) for b in marks]
+        outs = []
+        for own, _, q, k, v, packed in taken:
+            grad = causal_product(own, with_ones(v), turned(k, trig_s[...]), tri_s)
+            grad = (grad + dot_nt(own, spread_state(packed))) * trig_s[...]
+            outs.append(((grad[:, :PAIR] + grad[:, PAIR:]) * soft_slope(q)).astype(bf16))
+        for b, out in zip(marks, outs):
+            slope[block_of(b)] = out
+        return carry
+
+    for part in range(blocks // 2):
+        lax.fori_loop(part, part + 1, query_grad, 0)
+        engine.tick(2.6)
+    x_t_in.wait()
+    for t in range(3):
+        outer(0, 256 * t, slope[:, 256 * t : 256 * t + 256])
+    reduce.launch(next(shares))
+    engine.until("state")
+
+    def key_grad(b, carry):
+        own, num, q, k, v = take(b)
+        queries, keys = turned(q, trig_s[...]), turned(k, trig_s[...])
+        spread = spread_state(state.total(b).astype(bf16))
+        grad = causal_transposed(own, with_ones(v), queries, tri_s)
+        one = (lane_in_head(v.shape) == 0).astype(f32).astype(bf16)
+        grad = (grad + dot_nt(jnp.concatenate([v, one], axis=1), spread)) * trig_s[...]
+        grad = (grad[:, :PAIR] + grad[:, PAIR:]) * soft_slope(k)
+        grad_v = causal_transposed(queries, keys, num, tri_s) + dot(keys, spread[:, :PAIR])
+        rows, _ = block_of(b)
+        slope[rows, column_of(b, 1)] = grad.astype(bf16)
+        slope[rows, column_of(b, 2)] = grad_v.astype(bf16)
+        return carry
+
+    def group_of(t):
+        def body(i, carry):
+            return key_grad((i // 2) * 6 + t * 2 + lax.rem(i, 2), carry)
+
+        return body
+
+    for t in range(3):
+        for part in range(blocks // 3):
+            lax.fori_loop(part, part + 1, group_of(t), 0)
+            engine.tick(2.3)
+        for j in (1, 2):
+            outer(j, 256 * t, slope[:, D * j + 256 * t : D * j + 256 * t + 256])
+        reduce.launch(next(shares))
+    stores = [
+        pltpu.make_async_copy(slope.at[:, 0 : 3 * D], gp_o, load_sem.at[count[0]]),
+        pltpu.make_async_copy(norm_v, norm_o, load_sem.at[count[0] + 1]),
+        pltpu.make_async_copy(gr2, one_o, load_sem.at[count[0] + 2]),
+    ]
+    engine.until("norms")
+    for copy in stores:
+        copy.start()
+    engine.until(*[("sum", k) for k in range(SHARES)])
+    squares = Total(place, engine, "squares", sq_v, sq_w, sq_z, u_send, u_recv)
+    engine.until("squares")
+    stores.append(pltpu.make_async_copy(sq_v, square_o, load_sem.at[count[0] + 3]))
+    stores[3].start()
+    engine.rest()
+    wait(stores)
+    reduce.drain()
+    norms.drain()
+    squares.drain()
+    state.drain()
+
+
+def share_plan():
+    plan = [("down", 0, 8, 128 * t, 128) for t in range(3)]
+    plan += [("up", 0, 1, FF // 3 * t, FF // 3) for t in range(3)]
+    plan += [("attn", 3, 1, 0, D), ("attn", 0, 1, 0, D)]
+    plan += [("attn", 1, 2, 256 * t, 256) for t in range(3)]
+    return [part + (part[0] == "down", 1 if at % 2 else 2) for at, part in enumerate(plan)]
+
+
+SHARES = 11
+
+
+def backward_call(s, norm_params, seq_count):
+    rows = s["q"].shape[0]
+    blocks = rows // PIECE * 6
+    trig = turning_table(seq_count)
+    names = (
+        "wo", "wup", "q", "k", "v", "att", "rden", "xhat", "rstd", "x_t", "att_t",
+        "low_t", "act", "slope", "gb", "gb_t", "gr2", "state", "sums",
+    )
+    wdn = s["wdn"].reshape(4, PLANES, 2, 2, 48, D)
+    shapes = [
+        ((rows, 3 * D), bf16), ((rows, D), f32),
+        ((4, 2, 48, D), bf16), ((1, 2, 48, FF), bf16), ((8, 2, 48, FF // 8), bf16),
+        ((8, D), f32), ((8, 128), f32),
+    ]
+    vmem = [
+        ((D, FF), bf16), ((rows, FF), bf16), ((rows, FF), bf16), ((rows, D), f32),
+        ((rows, D), bf16), ((D, rows), bf16), ((rows, D), f32), ((rows, 128), f32),
+        ((4, PLANES, 2, 2, 48, D), bf16), ((8, PLANES, 2, 2, 48, FF // 8), bf16),
+        ((1, PLANES, 2, 2, 48, FF), bf16),
+        ((4, D), f32), ((PIECE, 2 * PAIR), f32), ((PIECE, PIECE // 2), bf16),
+        ((blocks, 144, PAIR), bf16), ((blocks, 144, PAIR), bf16), ((blocks, 144, PAIR), bf16),
+        ((blocks, 144, PAIR), bf16), ((blocks, 144, PAIR), bf16),
+        ((8, D), f32), ((8, 8, D), f32), ((PLANES, 8, D), f32),
+        ((8, 128), f32), ((8, 8, 128), f32), ((PLANES, 8, 128), f32),
+    ]
+    for _, _, units, _, width, by_units, early in share_plan():
+        count, part = (units // 2, width) if by_units else (units, width // 2)
+        vmem += [
+            ((units, PLANES, 2, 48, width), bf16), ((count, PLANES, 48, part), bf16),
+            ((count, PLANES, 48, part), bf16), ((count, early, 48, part), bf16),
+            ((count, PLANES - early, 48, part), bf16), ((count, 3, 48, part), bf16),
+            ((units, 2, 48, width), bf16),
+        ]
+    dma = pltpu.SemaphoreType.DMA
+    sems = [(36,), (SHARES,), (SHARES, 12), (SHARES, 12), (3,), (3,), (10,), (10,), (10,), (10,)]
+    hbm = pl.BlockSpec(memory_space=pl.ANY)
+    return pl.pallas_call(
+        backward_kernel,
+        out_shape=[jax.ShapeDtypeStruct(*shape) for shape in shapes],
+        in_specs=[hbm] * 22,
+        out_specs=[hbm] * len(shapes),
+        scratch_shapes=[pltpu.VMEM(*shape) for shape in vmem] + [dma(shape) for shape in sems],
+        compiler_params=pltpu.CompilerParams(
+            collective_id=1, has_side_effects=True, vmem_limit_bytes=VMEM_BYTES
+        ),
+        name="backward_reduce",
+    )(*[s[name] for name in names], wdn, norm_params, trig)
+
+
+def adam_step(weight, grad, first, second, rate, outs):
+    first_new = beta_one * first + (1.0 - beta_one) * grad
+    second_new = beta_two * second + (1.0 - beta_two) * grad * grad
+    first_hat = first_new * (1.0 / (1.0 - beta_one**STEP))
+    second_hat = second_new * (1.0 / (1.0 - beta_two**STEP))
+    step = first_hat / (jnp.sqrt(second_hat) + epsilon) + weight_decay * weight
+    grad_o, new_o, first_o, second_o = outs
+    grad_o[...] = grad
+    new_o[...] = weight - rate * step
+    first_o[...] = first_new
+    second_o[...] = second_new
+
+
+def update_kernel(
+    out_rate,
+    attn_r, up_r, down_r, norm_r, square_r,
+    attn_w, up_w, down_w, norm_w, attn_m, up_m, down_m, norm_m, attn_v, up_v, down_v, norm_v,
+    attn_g, up_g, down_g, norm_g, grad_norm_o,
+    attn_n, up_n, down_n, norm_n, attn_f, up_f, down_f, norm_f, attn_s, up_s, down_s, norm_s,
+    grad_s, turned_s,
+):
+    norm_raw = norm_r[0:4, :]
+    @pl.when(pl.program_id(0) == 0)
+    def _():
+        turned_s[...] = down_r[...].T.astype(f32)
+
+    grad_norm = jnp.sqrt(
+        jnp.sum(square_r[...], keepdims=True) + jnp.sum(norm_raw * norm_raw, keepdims=True)
+    )
+    clip = clip_limit / jnp.maximum(grad_norm, clip_limit)
+    grad_norm_o[...] = grad_norm
+    down_rate = learn_rate * math.sqrt(D / FF)
+    grad = up_r[...].astype(f32) * clip
+    adam_step(up_w[...], grad, up_m[...], up_v[...], learn_rate, (up_g, up_n, up_f, up_s))
+    rows = down_w.shape[0]
+    grad = turned_s[ds(pl.program_id(0) * rows, rows, rows), :] * clip
+    outs = (down_g, down_n, down_f, down_s)
+    adam_step(down_w[...], grad, down_m[...], down_v[...], down_rate, outs)
+    for j in range(4):
+        grad_s[:, j, :] = attn_r[j].astype(f32)
+    shape = grad_s.shape
+    rate = jnp.where(
+        lax.broadcasted_iota(jnp.int32, shape, 1) == 3, learn_rate * out_rate, learn_rate
+    )
+    grad = grad_s[...] * clip.reshape(1, 1, 1)
+    adam_step(attn_w[...], grad, attn_m[...], attn_v[...], rate, (attn_g, attn_n, attn_f, attn_s))
+    outs = (norm_g, norm_n, norm_f, norm_s)
+    adam_step(norm_w[...], norm_raw * clip, norm_m[...], norm_v[...], gain_rate, outs)
+
+
+def update_call(raw, norm_raw, square, weights, firsts, seconds, length):
+    steps = 6
+    thin, thick = weights[0].shape[0], weights[2].shape[0]
+    a, u, d = thin // steps, thin // steps, thick // steps
+    attn = pl.BlockSpec((a, 4, D), lambda t: (t, 0, 0))
+    up = pl.BlockSpec((u, FF), lambda t: (t, 0))
+    down = pl.BlockSpec((d, D), lambda t: (t, 0))
+    whole = lambda rows, cols: pl.BlockSpec((rows, cols), lambda t: (0, 0))
+    norm = whole(4, D)
+    kinds = [attn, up, down, norm]
+    shapes = [jax.ShapeDtypeStruct(w.shape, f32) for w in weights]
+    one = jax.ShapeDtypeStruct((1, 1), f32)
+    return pl.pallas_call(
+        functools.partial(update_kernel, math.sqrt(length // 8)),
+        grid=(steps,),
+        in_specs=[pl.BlockSpec((4, a, D), lambda t: (0, t, 0)), up, whole(D, thick)]
+        + [whole(8, D), whole(8, 128)]
+        + kinds * 3,
+        out_specs=kinds + [whole(1, 1)] + kinds * 3,
+        out_shape=shapes + [one] + shapes * 3,
+        scratch_shapes=[
+            pltpu.VMEM((a, 4, D), f32), pltpu.VMEM((thick, D), f32),
+        ],
+        compiler_params=pltpu.CompilerParams(vmem_limit_bytes=VMEM_BYTES),
+        name="adamw_update",
+    )(*raw, norm_raw, square, *weights, *firsts, *seconds)
+
+
 def prefix(part, axis, combine, identity):
     place = lax.axis_index(axis)
     gathered = jax.tree.map(lambda a: lax.all_gather(a, axis), part)
@@ -89,7 +1506,7 @@
     return (weight_new, first_new, second_new)
 
 
-def shards(
+def plain_shards(
     layer_input,
     cotangent,
     attn_master,
@@ -447,6 +1864,41 @@
     )
 
 
+def fused_shards(
+    layer_input, cotangent, attn_master, up_master, down_master, norm_params,
+    attn_first, up_first, down_first, norm_first,
+    attn_second, up_second, down_second, norm_second,
+):
+    groups, piece_rows, model_width = layer_input.shape
+    seq_count = lax.axis_size("seq")
+    rows = groups * piece_rows
+    weights = (attn_master, up_master, down_master, norm_params)
+    saved = forward_call(
+        layer_input.reshape(rows, model_width), *weights, seq_count,
+    )
+    saved |= second_norm(saved, cotangent.reshape(rows, model_width), norm_params)
+    gp, one, attn, up, down, norm_raw, square = backward_call(saved, norm_params, seq_count)
+    input_grad = input_call(gp, saved["wqkv"], one)
+    raw = (attn.reshape(4, -1, D), up.reshape(-1, FF), down.reshape(D, -1))
+    outs = update_call(
+        raw, norm_raw, square, weights,
+        (attn_first, up_first, down_first, norm_first),
+        (attn_second, up_second, down_second, norm_second), piece_rows * seq_count,
+    )
+    return (
+        saved["out"].reshape(layer_input.shape), input_grad.reshape(layer_input.shape),
+        *outs[:4], outs[4].reshape(()), *outs[5:],
+    )
+
+
+def shards(*args):
+    groups, piece_rows, model_width = args[0].shape
+    planes = lax.axis_size("dp") // 2
+    if piece_rows == PIECE and planes == PLANES and lax.axis_size("seq") == 4:
+        return fused_shards(*args)
+    return plain_shards(*args)
+
+
 def solution(mesh):
     in_specs = (
         P("dp", "seq", None),

time: 1040 us -> 245 us (0.24)
  waiting for transfers between devices: 509 us -> 0 us
  Pallas kernels: 0 us -> 240 us
  matrix products: 223 us -> 0 us
  local copies, waits for them, and re-layouts: 133 us -> 0 us
  blocking collectives: 73 us -> 0 us
  other arithmetic: 68.6 us -> 0 us
  between operations: 20.9 us -> 1.2 us
    pallas_call x0 -> x5, Pallas kernels: none -> 240 us  [the longest x1 117 us: backward_call(): pl.pallas_call(backward_kernel, out_shape=[jax.ShapeDtypeStruct(*shape) f...]
    dot_general x56 -> x0, matrix products: 223 us -> none  [the longest x2 26.6 us: piece_scores(): jnp.einsum('ihe,jhe->hij', query_cos, key_cos, preferred_element_type=jnp...]
    reduce_scatter x2 -> x0, waiting for transfers between devices: 195 us -> none  [the longest x1 98.7 us: shards(): lax.psum_scatter(grad_up.astype(jnp.bfloat16), 'dp', scatter_dimension=0,...]
    all_gather x5 -> x0, waiting for transfers between devices: 167 us -> none  [the longest x1 83.7 us: shards(): lax.all_gather(attn_master.astype(jnp.bfloat16), 'dp', axis=0, tiled=True)]
    unnamed x10 -> x0, waiting for transfers between devices: 139 us -> none
    psum x2 -> x0, blocking collectives: 62.4 us -> none  [the longest x1 40.7 us: shards(): norm_grad_raw = lax.psum(norm_grad_local, ('dp', 'seq'))]
    slice x20 -> x0, local copies, waits for them, and re-layouts: 39.3 us -> none  [the longest x3 7.2 us: shards(): values[group_index]]
    reshape x12 -> x0, local copies, waits for them, and re-layouts: 33.1 us -> none  [the longest x1 8.56 us: shards(): grad_in.reshape(model_width, 3, model_width)]
  transfers between devices with their start and end apart: 9 -> 0, of which waited for: 7 -> 0; matrix products, arithmetic and copies ran while one was open for 19% -> 0% of each run, Pallas kernels for 0% -> 0%
where the time goes in v1:
time: 245 us; the launch traced here: 241 us
  Pallas kernels  240 us (98%)
    pallas_call x1, Pallas kernels, backward_call(): pl.pallas_call(backward_kernel, out_shape=[jax.ShapeDtypeStruct(*shape) f...  117 us
    pallas_call x1, Pallas kernels, forward_call(): pl.pallas_call(forward_kernel, out_shape=out_shape, in_specs=[hbm] * 6, o...  87.5 us
    pallas_call x1, Pallas kernels, second_norm(): pl.pallas_call(second_norm_kernel, grid=(rows // tile,), in_specs=[by_row...  14.7 us
    pallas_call x1, Pallas kernels, update_call(): pl.pallas_call(functools.partial(update_kernel, math.sqrt(length // 8)),...  12.6 us
    pallas_call x1, Pallas kernels, input_call(): pl.pallas_call(input_kernel, grid=(rows // tile,), in_specs=[by_rows(3 *...  8.43 us

profile of v1, /device:TPU:0, one launch (start us, length us, event | category | flops | bytes accessed | tf_op | source)
XLA Modules:
  0.0 241.1 jit_solution(14556475974395347386)
XLA Ops:
  0.7 87.5 %gather_forward.1 = (bf16[768,2304]{1,0:T(8,128)(2,1)}, bf16[768,768]{1,0:T(8,128)(2,1)}, bf16[768,3072]{1,0:T(8,128)(2,1)}, bf16[3072,768]{1,0:T(8,128)(2,1)}, ...) custom-call(bf16[1024,768]{1,0:T(8,128)(2,1)} %bitcast.11, ...), custom_call_target="tpu_custom_call" | custom-call | tf_op jit(solution)/shard_map/gather_forward/pallas_call | solution.py:641
  88.2 14.7 %second_norm.1 = (bf16[1024,768]{1,0:T(8,128)(2,1)}, bf16[1024,768]{1,0:T(8,128)(2,1)}, bf16[768,1024]{1,0:T(8,128)(2,1)}, f32[1024,768]{1,0:T(8,128)}, f32[8,768]{1,0:T(8,128)}) custom-call(bf16[1024,3072]{1,0:T(8,128)(2,1)} %get-tuple-element.65.act.act_h, bf16[3072,768]{1,0:T(8,128)(2,1)} %get-tuple-element.66.wdn, ...), custom_call_target="tpu_custom_call" | custom-call | tf_op jit(solution)/shard_map/second_norm/pallas_call | solution.py:694
  102.9 116.7 %backward_reduce.1 = (bf16[1024,2304]{1,0:T(8,128)(2,1)}, f32[1024,768]{1,0:T(8,128)}, bf16[4,2,48,768]{3,2,1,0:T(8,128)(2,1)}, bf16[1,2,48,3072]{3,2,1,0:T(8,12...) custom-call(bf16[768,768]{1,0:T(8,128)(2,1)} %get-tuple-element.69.wo_h, ...), custom_call_target="tpu_custom_call" | custom-call | tf_op jit(solution)/shard_map/backward_reduce/pallas_call | solution.py:1351
  219.6 8.4 %input_gradient.1 = f32[1024,768]{1,0:T(8,128)} custom-call(bf16[1024,2304]{1,0:T(8,128)(2,1)} %get-tuple-element.86.gp, bf16[768,2304]{1,0:T(8,128)(2,1)} %get-tuple-element.87.w, f32[1024,768]{1,0:T(8,128)} %get-tuple-element.88.part), custom_call_target="tpu_custom_call" | custom-call | tf_op jit(solution)/shard_map/input_gradient/pallas_call | solution.py:724
  228.0 12.6 %adamw_update.1 = (f32[96,4,768]{2,1,0:T(4,128)}, f32[96,3072]{1,0:T(8,128)}, f32[384,768]{1,0:T(8,128)}, f32[4,768]{1,0:T(4,128)}, f32[1,1]{1,0:T(1,128)}, /*in...) custom-call(bf16[4,96,768]{2,1,0:T(8,128)(2,1)} %bitcast.13, ...), custom_call_target="tpu_custom_call" | custom-call | tf_op jit(solution)/shard_map/adamw_update/pallas_call | solution.py:1426

commit v2 on v1

--- a/solution.py
+++ b/solution.py
@@ -261,6 +261,11 @@
 
     def piece(self, k, z, y, x, c):
         ref, stride, base, height, column, width = self.chunks[k]
+        if stride is None:
+            return ref.at[
+                z * 2 + y, base, ds(c * height, height, 16),
+                pl.ds(pl.multiple_of(column + x * width, 128), width),
+            ]
         row = (z * 2 + y) * stride + base + c * height
         return ref.at[
             pl.ds(pl.multiple_of(row, 16), height),
@@ -412,8 +417,8 @@
         (wo, thin, 0, thin // 2, 0, D // 2),
         (wup, thin, 0, thin // 2, 0, FF // 4),
         (wup, thin, 0, thin // 2, FF // 2, FF // 4),
-        (wdn, thick, 0, thick // 4, 0, D // 2),
-        (wdn, thick, thick // 2, thick // 4, 0, D // 2),
+        (wdn, None, 0, thick // 4, 0, D // 2),
+        (wdn, None, 1, thick // 4, 0, D // 2),
     ]
     def ready(k):
         narrow = ds(shard * thin, thin, 32)
@@ -428,7 +433,7 @@
             wup[narrow, :] = up_st[...].astype(bf16)
         elif k == 5:
             loads[2].wait()
-            wdn[ds(shard * thick, thick, 128), :] = down_st[...].astype(bf16)
+            wdn[shard] = down_st[...].astype(bf16).reshape(2, thick // 2, D)
 
     engine = Engine()
     gather = Gather(place, engine, chunks, g_send, g_recv, ready)
@@ -582,6 +587,9 @@
         active = value * half
         slope = half + active * (1.0 - curve) * (scale + (3.0 * scale * 0.044715) * squared)
         act_s[:, 256 * t : 256 * t + 256] = active.astype(bf16)
+        if t % 3 == 2:
+            span = slice(256 * t - 512, 256 * t + 256)
+            store(act_s.at[:, span], act_o.at[:, span])
         slopes[t % 2][...] = slope.astype(bf16)
         slope_copy(t).start()
 
@@ -592,9 +600,10 @@
         return dot(low_s[...], wup[:, 256 * t : 256 * t + 256])
 
     chain([functools.partial(raised, t) for t in range(FF // 256)], expand, 1.1)
-    store(act_s, act_o)
-    engine.until(5, 6)
-    store(wdn, wdn_o)
+    engine.until(5)
+    store(wdn.at[:, 0], wdn_o.at[:, 0])
+    engine.until(6)
+    store(wdn.at[:, 1], wdn_o.at[:, 1])
     for copy in stores + [slope_copy(10), slope_copy(11)]:
         copy.wait()
     gather.drain()
@@ -607,7 +616,7 @@
     thin, thick = attn_master.shape[0], down_master.shape[0]
     trig = turning_table(seq_count)
     shapes = dict(
-        wqkv=((D, 3 * D), bf16), wo=((D, D), bf16), wup=((D, FF), bf16), wdn=((FF, D), bf16),
+        wqkv=((D, 3 * D), bf16), wo=((D, D), bf16), wup=((D, FF), bf16), wdn=((FF // thick, 2, thick // 2, D), bf16),
         q=((rows, D), bf16), k=((rows, D), bf16), v=((rows, D), bf16), att=((rows, D), bf16),
         rden=((rows, D), f32), xhat=((rows, D), f32), rstd=((rows, 128), f32),
         x_t=((D, rows), bf16), att_t=((D, rows), bf16), low_t=((D, rows), bf16),
@@ -617,7 +626,7 @@
     hbm = pl.BlockSpec(memory_space=pl.ANY)
     scratch = [
         pltpu.VMEM((D, 3 * D), bf16), pltpu.VMEM((D, D), bf16),
-        pltpu.VMEM((D, FF), bf16), pltpu.VMEM((FF, D), bf16),
+        pltpu.VMEM((D, FF), bf16), pltpu.VMEM((FF // thick, 2, thick // 2, D), bf16),
         pltpu.VMEM((thin, 4, D), f32), pltpu.VMEM((thin, FF), f32), pltpu.VMEM((thick, D), f32),
         pltpu.VMEM((rows, D), bf16), pltpu.VMEM((4, D), f32),
         pltpu.VMEM((PIECE, 2 * PAIR), f32), pltpu.VMEM((PIECE, PIECE // 2), bf16),
@@ -630,7 +639,7 @@
         pltpu.VMEM((D, rows), bf16), pltpu.VMEM((D, rows), bf16), pltpu.VMEM((D, rows), bf16),
         pltpu.VMEM((blocks, 144, PAIR), bf16), pltpu.VMEM((blocks, 144, PAIR), bf16),
         pltpu.VMEM((blocks, 144, PAIR), bf16), pltpu.VMEM((blocks, 144, PAIR), bf16),
-        pltpu.SemaphoreType.DMA((8,)), pltpu.SemaphoreType.DMA((21,)),
+        pltpu.SemaphoreType.DMA((8,)), pltpu.SemaphoreType.DMA((24,)),
         pltpu.SemaphoreType.DMA((2,)),
         pltpu.SemaphoreType.DMA((7, 28)), pltpu.SemaphoreType.DMA((7, 28)),
         pltpu.SemaphoreType.DMA((3,)), pltpu.SemaphoreType.DMA((3,)),
@@ -707,29 +716,8 @@
         scratch_shapes=[pltpu.VMEM((tile, D), f32)],
         compiler_params=pltpu.CompilerParams(vmem_limit_bytes=VMEM_BYTES),
         name="second_norm",
-    )(s["act"], s["wdn"], s["xhat"], cotangent, norm_params)
+    )(s["act"], s["wdn"].reshape(FF, D), s["xhat"], cotangent, norm_params)
     return dict(zip(("out", "gb", "gb_t", "gr2", "sums"), outs))
-
-
-def input_kernel(gp, w, part, out):
-    for column in range(0, D, 256):
-        cols = slice(column, column + 256)
-        out[:, cols] = part[:, cols] + dot_nt(gp[...], w[cols, :])
-
-
-def input_call(gp, w, part):
-    rows = part.shape[0]
-    tile = rows // 2
-    by_rows = lambda width: pl.BlockSpec((tile, width), lambda t: (t, 0))
-    return pl.pallas_call(
-        input_kernel,
-        grid=(rows // tile,),
-        in_specs=[by_rows(3 * D), pl.BlockSpec((D, 3 * D), lambda t: (0, 0)), by_rows(D)],
-        out_specs=by_rows(D),
-        out_shape=jax.ShapeDtypeStruct((rows, D), f32),
-        compiler_params=pltpu.CompilerParams(vmem_limit_bytes=VMEM_BYTES),
-        name="input_gradient",
-    )(gp, w, part)
 
 
 def turning_table(seq_count):
@@ -756,13 +744,6 @@
     def part(self, x):
         first, lanes = self.side(x)
         return pl.ds(first, self.count), lanes
-
-
-def add_into(target, at, other, there, more=None, where=None):
-    total = target[at].astype(f32) + other[there].astype(f32)
-    if more is not None:
-        total = total + more[where].astype(f32)
-    target[at] = total.astype(bf16)
 
 
 class Reduce:
@@ -814,16 +795,8 @@
     def fold_core(self, k, s):
         p = self.place
         self.pull(k, 0, s.twin)
-
-        def body(i, carry):
-            u, z = i // PLANES, lax.rem(i, PLANES)
-            for y in range(2):
-                own = s.grad[s.first + u, z, y, p.c, :, s.column : s.column + s.width]
-                total = s.twin[u, z, y].astype(f32) + own.astype(f32)
-                s.twin[u, z, y] = total.astype(bf16)
-            return carry
-
-        lax.fori_loop(0, PLANES * s.units, body, 0)
+        own = s.grad[s.first : s.first + s.units, :, :, p.c, :, s.column : s.column + s.width]
+        s.twin[...] = (s.twin[...].astype(f32) + own.astype(f32)).astype(bf16)
         e, oy, t = s.early, 1 - p.y, s.twin
         (mine, near), (theirs, far) = s.part(p.x), s.part(1 - p.x)
         self.push(k, 1, t.at[theirs, 0:e, oy, :, far], s.via_x, p.across_x(), "x")
@@ -839,23 +812,12 @@
         p, e, t, oy = self.place, s.early, s.twin, 1 - self.place.y
         (mine, near), (theirs, far) = s.part(p.x), s.part(1 - p.x)
         self.pull(k, 1, s.via_x)
-
-        def from_x(u, carry):
-            for z in range(e):
-                add_into(t, (s.side(p.x)[0] + u, z, oy, slice(None), near), s.via_x, (u, z))
-            return carry
-
-        lax.fori_loop(0, s.count, from_x, 0)
+        at = (mine, slice(0, e), oy, slice(None), near)
+        t[at] = (t[at].astype(f32) + s.via_x[...].astype(f32)).astype(bf16)
         self.push(k, 5, t.at[mine, 0:e, oy, :, near], s.from_y.at[:, 0:e], p.across_y(), "y")
         self.pull(k, 2, s.via_y)
-
-        def from_y(u, carry):
-            for z in range(e, PLANES):
-                at = (s.side(1 - p.x)[0] + u, z, p.y, slice(None), far)
-                add_into(t, at, s.via_y, (u, z - e))
-            return carry
-
-        lax.fori_loop(0, s.count, from_y, 0)
+        at = (theirs, slice(e, PLANES), p.y, slice(None), far)
+        t[at] = (t[at].astype(f32) + s.via_y[...].astype(f32)).astype(bf16)
         self.push(
             k, 6, t.at[theirs, e:PLANES, p.y, :, far], s.from_x.at[:, e:PLANES], p.across_x(), "x"
         )
@@ -867,14 +829,9 @@
         self.pull(k, 4, s.from_y.at[:, e:PLANES])
         self.pull(k, 5, s.from_y.at[:, 0:e])
         self.pull(k, 6, s.from_x.at[:, e:PLANES])
-
-        def body(i, carry):
-            u, z = i // PLANES, lax.rem(i, PLANES)
-            at = (s.side(p.x)[0] + u, z, p.y, slice(None), near)
-            add_into(t, at, s.from_x, (u, z), s.from_y, (u, z))
-            return carry
-
-        lax.fori_loop(0, PLANES * s.count, body, 0)
+        at = (mine, slice(None), p.y, slice(None), near)
+        total = t[at].astype(f32) + s.from_x[...].astype(f32) + s.from_y[...].astype(f32)
+        t[at] = total.astype(bf16)
         for step in (1, 3, 2):
             z = p.plane(step)
             self.push(
@@ -887,21 +844,15 @@
         mine, near = s.part(p.x)
         for step in (1, 3, 2):
             self.pull(k, 6 + step, s.planes.at[:, step - 1])
-
-        def body(u, carry):
-            at = s.side(p.x)[0] + u
-            total = s.twin[at, p.z, p.y, :, near].astype(f32)
-            for step in range(3):
-                total = total + s.planes[u, step].astype(f32)
-            total = total.astype(bf16)
-            s.final[at, p.c, :, near] = total
-            wide = total.astype(f32)
-            for lane in range(0, s.half, 128):
-                part = wide[:, lane : lane + 128]
-                self.squares[...] += jnp.sum((part * part).reshape(-1, 8, 128), axis=0)
-            return carry
-
-        lax.fori_loop(0, s.count, body, 0)
+        total = s.twin[mine, p.z, p.y, :, near].astype(f32)
+        for step in range(3):
+            total = total + s.planes[:, step].astype(f32)
+        total = total.astype(bf16)
+        s.final[mine, p.c, :, near] = total
+        wide = total.astype(f32).reshape(s.count * 48, s.half)
+        for lane in range(0, s.half, 128):
+            part = wide[:, lane : lane + 128]
+            self.squares[...] += jnp.sum((part * part).reshape(-1, 8, 128), axis=0)
         piece = s.final.at[mine, p.c, :, near]
         self.push(k, 10, piece, piece, p.across_x(), "x")
 
@@ -1048,9 +999,9 @@
 
 
 def backward_kernel(
-    wo_h, wup_h, q_h, k_h, v_h, att_h, rden_h, xhat_h, rstd_h, x_t_h, att_t_h,
+    wqkv_h, wo_h, wup_h, q_h, k_h, v_h, att_h, rden_h, xhat_h, rstd_h, x_t_h, att_t_h,
     low_t_h, act_h, slope_h, gb_h, gb_t_h, gr2_h, state_h, sums_h, wdn_h, norm_h, trig_h,
-    gp_o, one_o, attn_o, up_o, down_o, norm_o, square_o,
+    input_o, attn_o, up_o, down_o, norm_o, square_o,
     wup, acts, slope, gr2, gb, left, wide, rstd, ga_s, gd_s, gu_s,
     norm_s, trig_s, tri_s, state_s, st_own, st_twin, st_chip, st_prior,
     norm_v, norm_w, norm_z, sq_v, sq_w, sq_z,
@@ -1077,15 +1028,6 @@
 
     first_in = [load(gb_t_h, wup.at[:, 0:rows_all])]
     act_in = [load(act_h.at[:, D * z : D * z + D], acts.at[:, D * z : D * z + D]) for z in range(4)]
-    next_in = [load(gb_h, gb), load(wdn_h, ga_s), load(slope_h, slope), load(low_t_h, left)]
-    mid_in = [
-        load(gr2_h, gr2), load(xhat_h, wide), load(rstd_h, rstd), load(norm_h, norm_s),
-        load(sums_h, norm_v),
-    ]
-    late_in = [
-        load(state_h, state_s),
-        load(trig_h.at[ds((place.x * 2 + place.c) * PIECE, PIECE, PIECE), :], trig_s),
-    ]
     sq_v[...] = jnp.zeros_like(sq_v)
     fill_triangles(tri_s)
     engine = Engine(0.75)
@@ -1104,6 +1046,10 @@
         for z in range(PLANES):
             if t == 0:
                 act_in[z].wait()
+            if t == 0 and z == PLANES - 1:
+                next_in = [
+                    load(gb_h, gb), load(wdn_h, ga_s), load(slope_h, slope), load(low_t_h, left),
+                ]
             starts = [D * z + 384 * y + 128 * t for y in range(2)]
             pair = [acts[:, start : start + 128] for start in starts]
             part = dot(wup[:, 0:rows_all], jnp.concatenate(pair, axis=1)).astype(bf16)
@@ -1113,7 +1059,14 @@
             engine.tick(0.6)
         reduce.launch(next(shares))
 
-    mid_in.append(load(wup_h, wup))
+    mid_in = [
+        load(wup_h, wup), load(gr2_h, gr2), load(xhat_h, wide), load(rstd_h, rstd),
+        load(norm_h, norm_s), load(sums_h, norm_v),
+    ]
+    late_in = [
+        load(state_h, state_s),
+        load(trig_h.at[ds((place.x * 2 + place.c) * PIECE, PIECE, PIECE), :], trig_s),
+    ]
     for at, src in enumerate((q_h, k_h, v_h, att_h)):
         late_in.append(load(src, acts.at[:, D * at : D * at + D]))
     wait(next_in)
@@ -1156,6 +1109,7 @@
         lax.fori_loop(part, part + 1, first_back, 0)
         engine.tick(2.2)
     wo_in = load(wo_h, wup.at[:, 3 * D : 4 * D])
+    wqkv_in = load(wqkv_h, wup.at[:, 0 : 3 * D])
     for part in range(0, rows_all // 128, 4):
         lax.fori_loop(part, part + 4, norm_part, 0)
         engine.tick(0.8)
@@ -1253,37 +1207,51 @@
     reduce.launch(next(shares))
     engine.until("state")
 
-    def key_grad(b, carry):
-        own, num, q, k, v = take(b)
-        queries, keys = turned(q, trig_s[...]), turned(k, trig_s[...])
-        spread = spread_state(state.total(b).astype(bf16))
-        grad = causal_transposed(own, with_ones(v), queries, tri_s)
-        one = (lane_in_head(v.shape) == 0).astype(f32).astype(bf16)
-        grad = (grad + dot_nt(jnp.concatenate([v, one], axis=1), spread)) * trig_s[...]
-        grad = (grad[:, :PAIR] + grad[:, PAIR:]) * soft_slope(k)
-        grad_v = causal_transposed(queries, keys, num, tri_s) + dot(keys, spread[:, :PAIR])
-        rows, _ = block_of(b)
-        slope[rows, column_of(b, 1)] = grad.astype(bf16)
-        slope[rows, column_of(b, 2)] = grad_v.astype(bf16)
-        return carry
-
-    def group_of(t):
-        def body(i, carry):
-            return key_grad((i // 2) * 6 + t * 2 + lax.rem(i, 2), carry)
+    def key_pair(t):
+        def body(g, carry):
+            marks = [g * 6 + 2 * t, g * 6 + 2 * t + 1]
+            taken = [take(b) + (state.total(b).astype(bf16),) for b in marks]
+            outs = []
+            for own, num, q, k, v, packed in taken:
+                queries, keys = turned(q, trig_s[...]), turned(k, trig_s[...])
+                spread = spread_state(packed)
+                grad = causal_transposed(own, with_ones(v), queries, tri_s)
+                one = (lane_in_head(v.shape) == 0).astype(f32).astype(bf16)
+                grad = (grad + dot_nt(jnp.concatenate([v, one], axis=1), spread)) * trig_s[...]
+                grad = (grad[:, :PAIR] + grad[:, PAIR:]) * soft_slope(k)
+                grad_v = causal_transposed(queries, keys, num, tri_s)
+                grad_v = grad_v + dot(keys, spread[:, :PAIR])
+                outs.append((grad.astype(bf16), grad_v.astype(bf16)))
+            for b, (grad, grad_v) in zip(marks, outs):
+                rows, _ = block_of(b)
+                slope[rows, column_of(b, 1)] = grad
+                slope[rows, column_of(b, 2)] = grad_v
+            return carry
 
         return body
 
     for t in range(3):
-        for part in range(blocks // 3):
-            lax.fori_loop(part, part + 1, group_of(t), 0)
-            engine.tick(2.3)
+        for part in range(blocks // 6):
+            lax.fori_loop(part, part + 1, key_pair(t), 0)
+            engine.tick(4.4)
         for j in (1, 2):
             outer(j, 256 * t, slope[:, D * j + 256 * t : D * j + 256 * t + 256])
         reduce.launch(next(shares))
+    wqkv_in.wait()
+
+    def input_grad(t, carry):
+        cols = ds(t * tile, tile, tile)
+        for part in range(0, rows_all, PIECE):
+            span = slice(part, part + PIECE)
+            gr2[span, cols] += dot_nt(slope[span, 0 : 3 * D], wup[cols, 0 : 3 * D])
+        return carry
+
+    for part in range(3):
+        lax.fori_loop(part, part + 1, input_grad, 0)
+        engine.tick(1.8)
     stores = [
-        pltpu.make_async_copy(slope.at[:, 0 : 3 * D], gp_o, load_sem.at[count[0]]),
+        pltpu.make_async_copy(gr2, input_o, load_sem.at[count[0]]),
         pltpu.make_async_copy(norm_v, norm_o, load_sem.at[count[0] + 1]),
-        pltpu.make_async_copy(gr2, one_o, load_sem.at[count[0] + 2]),
     ]
     engine.until("norms")
     for copy in stores:
@@ -1291,8 +1259,8 @@
     engine.until(*[("sum", k) for k in range(SHARES)])
     squares = Total(place, engine, "squares", sq_v, sq_w, sq_z, u_send, u_recv)
     engine.until("squares")
-    stores.append(pltpu.make_async_copy(sq_v, square_o, load_sem.at[count[0] + 3]))
-    stores[3].start()
+    stores.append(pltpu.make_async_copy(sq_v, square_o, load_sem.at[count[0] + 2]))
+    stores[2].start()
     engine.rest()
     wait(stores)
     reduce.drain()
@@ -1317,12 +1285,12 @@
     blocks = rows // PIECE * 6
     trig = turning_table(seq_count)
     names = (
-        "wo", "wup", "q", "k", "v", "att", "rden", "xhat", "rstd", "x_t", "att_t",
+        "wqkv", "wo", "wup", "q", "k", "v", "att", "rden", "xhat", "rstd", "x_t", "att_t",
         "low_t", "act", "slope", "gb", "gb_t", "gr2", "state", "sums",
     )
     wdn = s["wdn"].reshape(4, PLANES, 2, 2, 48, D)
     shapes = [
-        ((rows, 3 * D), bf16), ((rows, D), f32),
+        ((rows, D), f32),
         ((4, 2, 48, D), bf16), ((1, 2, 48, FF), bf16), ((8, 2, 48, FF // 8), bf16),
         ((8, D), f32), ((8, 128), f32),
     ]
@@ -1351,7 +1319,7 @@
     return pl.pallas_call(
         backward_kernel,
         out_shape=[jax.ShapeDtypeStruct(*shape) for shape in shapes],
-        in_specs=[hbm] * 22,
+        in_specs=[hbm] * 23,
         out_specs=[hbm] * len(shapes),
         scratch_shapes=[pltpu.VMEM(*shape) for shape in vmem] + [dma(shape) for shape in sems],
         compiler_params=pltpu.CompilerParams(
@@ -1375,16 +1343,20 @@
 
 
 def update_kernel(
-    out_rate,
-    attn_r, up_r, down_r, norm_r, square_r,
+    out_rate, steps,
+    input_h, attn_r, up_r, down_r, norm_r, square_r,
     attn_w, up_w, down_w, norm_w, attn_m, up_m, down_m, norm_m, attn_v, up_v, down_v, norm_v,
-    attn_g, up_g, down_g, norm_g, grad_norm_o,
+    input_o, attn_g, up_g, down_g, norm_g, grad_norm_o,
     attn_n, up_n, down_n, norm_n, attn_f, up_f, down_f, norm_f, attn_s, up_s, down_s, norm_s,
-    grad_s, turned_s,
+    grad_s, turned_s, input_s, copy_sem,
 ):
     norm_raw = norm_r[0:4, :]
+    inward = pltpu.make_async_copy(input_h, input_s, copy_sem.at[0])
+    outward = pltpu.make_async_copy(input_s, input_o, copy_sem.at[1])
+
     @pl.when(pl.program_id(0) == 0)
     def _():
+        inward.start()
         turned_s[...] = down_r[...].T.astype(f32)
 
     grad_norm = jnp.sqrt(
@@ -1410,8 +1382,17 @@
     outs = (norm_g, norm_n, norm_f, norm_s)
     adam_step(norm_w[...], norm_raw * clip, norm_m[...], norm_v[...], gain_rate, outs)
 
-
-def update_call(raw, norm_raw, square, weights, firsts, seconds, length):
+    @pl.when(pl.program_id(0) == 1)
+    def _():
+        inward.wait()
+        outward.start()
+
+    @pl.when(pl.program_id(0) == steps - 1)
+    def _():
+        outward.wait()
+
+
+def update_call(input_grad, raw, norm_raw, square, weights, firsts, seconds, length):
     steps = 6
     thin, thick = weights[0].shape[0], weights[2].shape[0]
     a, u, d = thin // steps, thin // steps, thick // steps
@@ -1423,20 +1404,22 @@
     kinds = [attn, up, down, norm]
     shapes = [jax.ShapeDtypeStruct(w.shape, f32) for w in weights]
     one = jax.ShapeDtypeStruct((1, 1), f32)
+    hbm = pl.BlockSpec(memory_space=pl.ANY)
     return pl.pallas_call(
-        functools.partial(update_kernel, math.sqrt(length // 8)),
+        functools.partial(update_kernel, math.sqrt(length // 8), steps),
         grid=(steps,),
-        in_specs=[pl.BlockSpec((4, a, D), lambda t: (0, t, 0)), up, whole(D, thick)]
+        in_specs=[hbm, pl.BlockSpec((4, a, D), lambda t: (0, t, 0)), up, whole(D, thick)]
         + [whole(8, D), whole(8, 128)]
         + kinds * 3,
-        out_specs=kinds + [whole(1, 1)] + kinds * 3,
-        out_shape=shapes + [one] + shapes * 3,
+        out_specs=[hbm] + kinds + [whole(1, 1)] + kinds * 3,
+        out_shape=[jax.ShapeDtypeStruct(input_grad.shape, f32)] + shapes + [one] + shapes * 3,
         scratch_shapes=[
             pltpu.VMEM((a, 4, D), f32), pltpu.VMEM((thick, D), f32),
+            pltpu.VMEM(input_grad.shape, f32), pltpu.SemaphoreType.DMA((2,)),
         ],
         compiler_params=pltpu.CompilerParams(vmem_limit_bytes=VMEM_BYTES),
         name="adamw_update",
-    )(*raw, norm_raw, square, *weights, *firsts, *seconds)
+    )(input_grad, *raw, norm_raw, square, *weights, *firsts, *seconds)
 
 
 def prefix(part, axis, combine, identity):
@@ -1877,11 +1860,10 @@
         layer_input.reshape(rows, model_width), *weights, seq_count,
     )
     saved |= second_norm(saved, cotangent.reshape(rows, model_width), norm_params)
-    gp, one, attn, up, down, norm_raw, square = backward_call(saved, norm_params, seq_count)
-    input_grad = input_call(gp, saved["wqkv"], one)
+    input_grad, attn, up, down, norm_raw, square = backward_call(saved, norm_params, seq_count)
     raw = (attn.reshape(4, -1, D), up.reshape(-1, FF), down.reshape(D, -1))
-    outs = update_call(
-        raw, norm_raw, square, weights,
+    input_grad, *outs = update_call(
+        input_grad, raw, norm_raw, square, weights,
         (attn_first, up_first, down_first, norm_first),
         (attn_second, up_second, down_second, norm_second), piece_rows * seq_count,
     )

time: 245 us -> 239 us (0.976)
  Pallas kernels: 240 us -> 233 us
    pallas_call x2 -> x1, Pallas kernels: 21 us -> 14 us  [update_call(): pl.pallas_call(functools.partial(update_kernel, math.sqrt(length // 8), s...]
where the time goes in v2:
time: 239 us; the launch traced here: 234 us
  Pallas kernels  233 us (97%)
    pallas_call x1, Pallas kernels, backward_call(): pl.pallas_call(backward_kernel, out_shape=[jax.ShapeDtypeStruct(*shape) f...  117 us
    pallas_call x1, Pallas kernels, forward_call(): pl.pallas_call(forward_kernel, out_shape=out_shape, in_specs=[hbm] * 6, o...  87 us
    pallas_call x1, Pallas kernels, second_norm(): pl.pallas_call(second_norm_kernel, grid=(rows // tile,), in_specs=[by_row...  14.7 us
    pallas_call x1, Pallas kernels, update_call(): pl.pallas_call(functools.partial(update_kernel, math.sqrt(length // 8), s...  14 us

profile of v2, /device:TPU:0, one launch (start us, length us, event | category | flops | bytes accessed | tf_op | source)
XLA Modules:
  0.0 234.2 jit_solution(15598903615135694370)
XLA Ops:
  0.7 87.0 %gather_forward.1 = (bf16[768,2304]{1,0:T(8,128)(2,1)}, bf16[768,768]{1,0:T(8,128)(2,1)}, bf16[768,3072]{1,0:T(8,128)(2,1)}, bf16[8,2,192,768]{3,2,1,0:T(8,128)(...) custom-call(bf16[1024,768]{1,0:T(8,128)(2,1)} %bitcast.12, ...), custom_call_target="tpu_custom_call" | custom-call | tf_op jit(solution)/shard_map/gather_forward/pallas_call | solution.py:650
  87.7 14.7 %second_norm.1 = (bf16[1024,768]{1,0:T(8,128)(2,1)}, bf16[1024,768]{1,0:T(8,128)(2,1)}, bf16[768,1024]{1,0:T(8,128)(2,1)}, f32[1024,768]{1,0:T(8,128)}, f32[8,768]{1,0:T(8,128)}) custom-call(bf16[1024,3072]{1,0:T(8,128)(2,1)} %get-tuple-element.65.act.act_h, bf16[3072,768]{1,0:T(8,128)(2,1)} %bitcast.10, f32[1024,768]{1,0:T(8,128)} %get-tuple-element.67.xhat.xhat_h, ...), custom_call_target="tpu_custom_call" | custom-call | tf_op jit(solution)/shard_map/second_norm/pallas_call | solution.py:703
  102.4 117.3 %backward_reduce.1 = (f32[1024,768]{1,0:T(8,128)}, bf16[4,2,48,768]{3,2,1,0:T(8,128)(2,1)}, bf16[1,2,48,3072]{3,2,1,0:T(8,128)(2,1)}, bf16[8,2,48,384]{3,2,1,0:T...) custom-call(bf16[768,2304]{1,0:T(8,128)(2,1)} %get-tuple-element.69.wqkv_h, bf16[768,768]{1,0:T(8,128)(2,1)} %get-tuple-element.70.wo_h, ...), custom_call_target="tpu_custom_call" | custom-call | tf_op jit(solution)/shard_map/backward_reduce/pallas_call | solution.py:1319
  219.7 14.0 %adamw_update.1 = (f32[1024,768]{1,0:T(8,128)}, f32[96,4,768]{2,1,0:T(4,128)}, f32[96,3072]{1,0:T(8,128)}, f32[384,768]{1,0:T(8,128)}, f32[4,768]{1,0:T(4,128)},...) custom-call(f32[1024,768]{1,0:T(8,128)} %get-tuple-element.87.input_, ...), custom_call_target="tpu_custom_call" | custom-call | tf_op jit(solution)/shard_map/adamw_update/pallas_call | solution.py:1408
